TPU v7x, 256 devices: a whole 4x4x8 slice. The times are simulated.
256 devices in a mesh: dp: 4 (over y), expert: 64 (over z, x, core).
Axes of the slice: x: 4, y: 4, z: 8, core: 2. Of those that a mesh axis runs over, the one named last changes fastest.
Arguments:
- grad_parts: bfloat16 [4, 512, 1536, 256], P('dp', None, 'expert'), may hold values from -6 to 6
- momentum: bfloat16 [512, 1536, 256], P('dp', 'expert'), may hold values from -6 to 6
- block_ids: int32 [512], P('dp'), may hold values from 0 to 511, each once
- step: int32 [1], replicated, may hold values from 0 to 9999
- logit_max: float32 [4, 64, 4, 64], P('dp', 'expert'), may hold values from 5 to 600, as said below
Outputs:
- new_momentum: bfloat16 [512, 1536, 256], P('dp', 'expert')
- update: bfloat16 [512, 1536, 256], P('dp', 'expert')
- clip_scale: float32 [512, 256], P('dp')
Inputs may be any that keep to these rules, and one draw needn't show every extreme that they name: `block_ids`: every slot number appears once. `logit_max`: positive.
All inputs are finite; a program needn't handle non-finite values.
Results may differ from a plain program's by a relative error of at most 0.02.
Values may be sent and summed in bfloat16 or wider, within the bound.
A program may use at most 64 MiB of HBM per device.

v0:
```python
import jax
import jax.numpy as jnp
from jax import lax
from jax.sharding import PartitionSpec as P

Q_IN = 1536
KV_IN = 512
NOPE_DIM = 128
NS_STEPS = 5
Q_OUT = 192
KV_OUT = 256


quintic_a = 3.4445
quintic_b = -4.775
quintic_c = 2.0315
norm_eps = 1e-07
beta_coef = 0.95
clip_tau = 100.0
plan_span = 10000.0
rms_match = 0.2
full_prec = lax.Precision.HIGHEST


def orthogonalize(direction):
    values = direction.astype(jnp.float32)
    squares = jnp.sum(jnp.square(values))
    current = values / (jnp.sqrt(squares) + norm_eps)
    for sweep_index in range(NS_STEPS):
        gram_matrix = lax.dot_general(
            current,
            current,
            (((0,), (0,)), ((), ())),
            precision=full_prec,
            preferred_element_type=jnp.float32,
        )
        polynomial = quintic_b * gram_matrix + quintic_c * jnp.dot(
            gram_matrix, gram_matrix, precision=full_prec, preferred_element_type=jnp.float32
        )
        current = quintic_a * current + jnp.dot(
            current, polynomial, precision=full_prec, preferred_element_type=jnp.float32
        )
    return current


def live_limits(block_kind):
    in_live = jnp.where(block_kind == 0, Q_IN, KV_IN)
    out_live = jnp.where(block_kind == 0, Q_OUT, KV_OUT)
    return (in_live, out_live)


def body(grad_parts, momentum, block_ids, step, logit_max):
    owners = lax.axis_size("expert")
    column = lax.axis_index("expert")
    slot_rows = momentum.shape[0]
    piece_rows = momentum.shape[1]
    slots_each = slot_rows // owners
    partial_value = grad_parts[0]
    summed = lax.psum_scatter(
        partial_value.astype(jnp.float32).astype(jnp.bfloat16),
        "dp",
        scatter_dimension=0,
        tiled=True,
    ).astype(jnp.float32)
    head_peaks = lax.pmax(logit_max[0, 0], ("dp", "expert"))
    step_rate = 0.1 + 0.45 * (1.0 + jnp.cos(jnp.pi * step[0].astype(jnp.float32) / plan_span))
    block_kind = block_ids % 2
    in_live, out_live = live_limits(block_kind)
    in_pos = column * piece_rows + jnp.arange(piece_rows)
    live_mask = (in_pos[None, :, None] < in_live[:, None, None]) & (
        jnp.arange(KV_OUT)[None, None, :] < out_live[:, None, None]
    )
    gradient = jnp.where(live_mask, summed, 0.0)
    send_order = jnp.arange(slot_rows, dtype=jnp.int32)
    own_slots = lax.dynamic_slice_in_dim(send_order, column * slots_each, slots_each, 0)
    own_kind = block_kind[own_slots]
    own_in, own_out = live_limits(own_kind)
    widest = jnp.where(own_kind == 0, max(Q_IN, Q_OUT), max(KV_IN, KV_OUT))
    scales = step_rate * rms_match * jnp.sqrt(widest.astype(jnp.float32))
    own_grad = lax.all_to_all(
        gradient.astype(jnp.bfloat16), "expert", split_axis=0, concat_axis=1, tiled=True
    ).astype(jnp.float32)
    own_held = lax.all_to_all(momentum, "expert", split_axis=0, concat_axis=1, tiled=True).astype(
        jnp.float32
    )
    own_mask = (jnp.arange(Q_IN)[None, :, None] < own_in[:, None, None]) & (
        jnp.arange(KV_OUT)[None, None, :] < own_out[:, None, None]
    )
    fresh_own = jnp.where(own_mask, beta_coef * own_held + own_grad, 0.0).astype(jnp.bfloat16)
    nesterov = (own_grad + beta_coef * fresh_own.astype(jnp.float32)).astype(jnp.bfloat16)
    orthogonal = lax.map(orthogonalize, nesterov)
    update_own = (scales[:, None, None] * orthogonal).astype(jnp.bfloat16)
    fresh_back, update_rows = (
        lax.all_to_all(fresh_own, "expert", split_axis=1, concat_axis=0, tiled=True),
        lax.all_to_all(update_own, "expert", split_axis=1, concat_axis=0, tiled=True),
    )
    clip_eta = jnp.minimum(1.0, clip_tau / head_peaks).reshape(-1)
    head_pair = block_ids // 2
    picker = head_pair[:, None] == jnp.arange(clip_eta.shape[0])[None, :]
    slot_eta = jnp.sum(jnp.where(picker, clip_eta[None, :], 0.0), axis=1)
    out_rows = jnp.arange(KV_OUT)[None, :]
    root_eta = jnp.sqrt(slot_eta)[:, None]
    query_rows = jnp.where(
        out_rows < NOPE_DIM, root_eta, jnp.where(out_rows < Q_OUT, slot_eta[:, None], 0.0)
    )
    value_rows = jnp.where(out_rows < NOPE_DIM, root_eta, 1.0)
    clip_scale = jnp.where((block_kind == 0)[:, None], query_rows, value_rows)
    return (fresh_back, update_rows, clip_scale)


def solution(mesh):
    in_specs = (
        P("dp", None, "expert", None),
        P("dp", "expert", None),
        P("dp"),
        P(),
        P("dp", "expert", None, None),
    )
    out_specs = (P("dp", "expert", None), P("dp", "expert", None), P("dp", None))
    return jax.shard_map(body, mesh=mesh, in_specs=in_specs, out_specs=out_specs, check_vma=False)
```

profile of v0, /device:TPU:1, one launch (start us, length us, event | category | flops | bytes accessed | tf_op | source)
XLA Modules:
  0.0 351.3 jit_solution(11909575946385385246)
XLA Ops:
  7.2 0.7 reduce-scatter.2.cloned.1.call-update
  7.9 13.0 %all-to-all-start = ((bf16[128,24,256]{2,1,0:T(8,128)(2,1)}), bf16[128,24,256]{2,1,0:T(8,128)(2,1)S(1)}, u32[]{:S(2)}, u32[]{:S(2)}) async-start(bf16[128,24,256]{2,1,0:T(8,128)(2,1)} %param.8), calls=%async_computation | async-start | bytes 3145728 | tf_op jit(solution)/shard_map/all_to_all | solution.py:83
  21.2 59.8 %reduce-scatter.2.cloned.1.call-done = bf16[128,24,256]{2,1,0:T(8,128)(2,1)} async-done(((bf16[512,24,256]{2,1,0:T(8,128)(2,1)}), bf16[128,24,256]{2,1,0:T(8,128)(2,1)}) %reduce-scatter.2.cloned.1.call-update) | async-done | bytes 1572880 | tf_op jit(solution)/shard_map/reduce_scatter | solution.py:59
  81.0 2.8 select_convert_fusion
  83.8 10.8 %all-to-all-start.1 = ((bf16[128,24,256]{2,1,0:T(8,128)(2,1)}), bf16[128,24,256]{2,1,0:T(8,128)(2,1)}, u32[]{:S(2)}, u32[]{:S(2)}) async-start(bf16[128,24,256]{2,1,0:T(8,128)(2,1)} %select_convert_fusion), calls=%async_computation.2 | async-start | bytes 3145728 | tf_op jit(solution)/shard_map/all_to_all | solution.py:80
  94.7 0.6 gather_fusion
  96.6 1.6 copy.23
  98.2 35.3 %all-to-all-done.1 = bf16[128,24,256]{2,1,0:T(8,128)(2,1)} async-done(((bf16[128,24,256]{2,1,0:T(8,128)(2,1)}), bf16[128,24,256]{2,1,0:T(8,128)(2,1)}, u32[]{:S(2)}, u32[]{:S(2)}) %all-to-all-start.1) | async-done | bytes 1572896 | tf_op jit(solution)/shard_map/all_to_all | solution.py:80
  133.5 2.6 copy.24
  136.1 7.3 %fusion.19 = (bf16[2,1536,256]{2,0,1:T(2,128)(2,1)S(1)}, bf16[2,1536,256]{2,0,1:T(2,128)(2,1)}) fusion(f32[64,2,24,256]{3,1,2,0:T(2,128)S(1)} %copy.24, f32[64,2,24,256]{3,1,2,0:T(2,128)S(1)} %copy.23, pred[2,256]{1,0:T(4,128)(4,1)S(1)} %iota_compare_fusion.3, pred[2,1536]{0,1:T(8,128)(4,1)S(1)} %iota_compare_fusion), kind=kLoop, calls=%fused_computation.33 | loop fusion | flops 6291456 | bytes 9440768 | tf_op jit(solution)/shard_map/convert_element_type | solution.py:90
  143.6 52.1 %while.10 = (s32[]{:T(128)}, f32[2,1536,256]{2,1,0:T(8,128)}, bf16[2,1536,256]{2,1,0:T(8,128)(2,1)S(1)}, s32[]{:T(128)}, f32[]{:T(128)}) while((s32[]{:T(128)}, f32[2,1536,256]{2,1,0:T(8,128)}, bf16[2,1536,256]{2,1,0:T(8,128)(2,1)S(1)}, s32[]{:T(128)}, f32[]{:T(128)}) %tuple.29), condition=%wide.region_3.4_spmd, body=%wide.region_1.3_spmd.sunk | while | flops 13094682624 | bytes 30411360 | solution.py:91
  143.8 1.0 fusion.122
  145.5 2.7 fusion.123
  148.3 0.4 fusion.124
  148.7 1.5 convolution_add_fusion.9
  150.1 2.8 fusion.125
  152.9 0.4 fusion.126
  153.3 1.5 convolution_add_fusion.10
  154.8 2.8 fusion.127
  157.6 0.4 fusion.128
  158.0 1.5 convolution_add_fusion.11
  159.4 2.8 fusion.129
  162.2 0.4 fusion.130
  162.6 1.5 convolution_add_fusion.12
  164.0 2.8 fusion.131
  166.8 0.4 fusion.132
  167.2 2.6 fusion.133
  169.8 1.0 fusion.122
  171.5 2.7 fusion.123
  174.2 0.4 fusion.124
  174.6 1.5 convolution_add_fusion.9
  176.1 2.8 fusion.125
  179.3 1.5 convolution_add_fusion.10
  180.7 2.8 fusion.127
  183.9 1.5 convolution_add_fusion.11
  185.4 2.8 fusion.129
  188.5 1.5 convolution_add_fusion.12
  190.0 2.8 fusion.131
  192.8 0.4 fusion.132
  193.2 2.6 fusion.133
  195.7 2.2 multiply_convert_fusion
  198.0 9.6 %copy.28 = bf16[2,1536,256]{2,0,1:T(2,128)(2,1)S(1)} copy(bf16[2,1536,256]{2,1,0:T(8,128)(2,1)S(1)} %multiply_convert_fusion) | data formatting | bytes 3145728 | tf_op jit(solution)/shard_map/convert_element_type | solution.py:92
  207.6 45.3 %all_to_all.54 = bf16[2,1536,256]{2,0,1:T(2,128)(2,1)S(1)} all-to-all(bf16[2,1536,256]{2,0,1:T(2,128)(2,1)S(1)} %copy.28), channel_id=1, replica_groups=mesh['dp'=4,'expert'=64] {'expert'}, dimensions={1} | all-to-all | bytes 3145728 | tf_op jit(solution)/shard_map/all_to_all | solution.py:95
  252.9 6.6 %all-to-all-start.2 = ((bf16[2,1536,256]{2,0,1:T(2,128)(2,1)}), bf16[2,1536,256]{2,0,1:T(2,128)(2,1)S(1)}, u32[]{:S(2)}, u32[]{:S(2)}) async-start(bf16[2,1536,256]{2,0,1:T(2,128)(2,1)} %get-tuple-element.36), calls=%async_computation.3 | async-start | bytes 3145728 | tf_op jit(solution)/shard_map/all_to_all | solution.py:94
  259.5 81.1 %pmax.7 = f32[4,64]{1,0:T(4,128)S(1)} all-reduce(f32[4,64]{1,0:T(4,128)S(1)} %bitcast.135), channel_id=1, replica_groups=mesh['dp'=4,'expert'=64] {'dp','expert'}, use_global_device_ids=true, to_apply=%region_4.5 | all-reduce | flops 256 | bytes 2048 | tf_op jit(solution)/shard_map/pmax | solution.py:65
  340.9 0.8 select_select_fusion
  341.6 1.4 copy.29
  343.0 1.4 copy.25
  (31 shorter events, 2.5 us)
Async XLA Ops:
  7.2 73.8 %reduce-scatter.2.cloned.1.call-start = ((), (), s32[]{:S(2)}) async-start(), calls=%async_computation.5 | async-start | bytes 7864320 | tf_op jit(solution)/shard_map/reduce_scatter | solution.py:59
  7.9 13.0 %copy-start.1 = (s32[128]{0:T(128)S(1)}, s32[128]{0:T(128)}, u32[]{:S(2)}) copy-start(s32[128]{0:T(128)} %param.9) | copy-start | bytes 1540
  7.9 75.9 %all-to-all-start = ((bf16[128,24,256]{2,1,0:T(8,128)(2,1)}), bf16[128,24,256]{2,1,0:T(8,128)(2,1)S(1)}, u32[]{:S(2)}, u32[]{:S(2)}) async-start(bf16[128,24,256]{2,1,0:T(8,128)(2,1)} %param.8), calls=%async_computation | async-start | bytes 3145728 | tf_op jit(solution)/shard_map/all_to_all | solution.py:83
  83.8 49.7 %all-to-all-start.1 = ((bf16[128,24,256]{2,1,0:T(8,128)(2,1)}), bf16[128,24,256]{2,1,0:T(8,128)(2,1)}, u32[]{:S(2)}, u32[]{:S(2)}) async-start(bf16[128,24,256]{2,1,0:T(8,128)(2,1)} %select_convert_fusion), calls=%async_computation.2 | async-start | bytes 3145728 | tf_op jit(solution)/shard_map/all_to_all | solution.py:80
  252.9 6.6 %copy-start = (f32[1,1,4,64]{3,2,1,0:T(4,128)S(1)}, f32[1,1,4,64]{3,2,1,0:T(4,128)}, u32[]{:S(2)}) copy-start(f32[1,1,4,64]{3,2,1,0:T(4,128)} %param.11) | copy-start | bytes 3076
  252.9 90.2 %all-to-all-start.2 = ((bf16[2,1536,256]{2,0,1:T(2,128)(2,1)}), bf16[2,1536,256]{2,0,1:T(2,128)(2,1)S(1)}, u32[]{:S(2)}, u32[]{:S(2)}) async-start(bf16[2,1536,256]{2,0,1:T(2,128)(2,1)} %get-tuple-element.36), calls=%async_computation.3 | async-start | bytes 3145728 | tf_op jit(solution)/shard_map/all_to_all | solution.py:94
Sparse Core Ops, SparseCore 0:
  10.6 70.3 reduce-scatter.1
where the time goes:
time: 352 us; the launch traced here: 351 us
  blocking collectives  126 us (36%)
  waiting for transfers between devices  95.8 us (27%)
  matrix products  48.3 us (14%)
  starting transfers between devices  30.4 us (9%)
  local copies, waits for them, and re-layouts  17.6 us (5%)
  other arithmetic  16.1 us (5%)
  between operations  14.9 us (4%)
    pmax x1, blocking collectives, body(): head_peaks = lax.pmax(logit_max[0, 0], ('dp', 'expert'))  81.1 us
    reduce_scatter x1, waiting for transfers between devices, body(): lax.psum_scatter(partial_value.astype(jnp.float32).astype(jnp.bfloat16),...  59.8 us
    all_to_all x1, blocking collectives, body(): lax.all_to_all(update_own, 'expert', split_axis=1, concat_axis=0, tiled=T...  45.3 us
    all_to_all x1, waiting for transfers between devices, body(): lax.all_to_all(gradient.astype(jnp.bfloat16), 'expert', split_axis=0, con...  35.3 us
    dot_general x10, matrix products, orthogonalize(): lax.dot_general(current, current, (((0,), (0,)), ((), ())), precision=ful...  27.7 us
    dot_general x10, matrix products, orthogonalize(): jnp.dot(current, polynomial, precision=full_prec, preferred_element_type=...  16.8 us
    all_to_all x1, starting transfers between devices, body(): lax.all_to_all(momentum, 'expert', split_axis=0, concat_axis=1, tiled=True)  13 us
    all_to_all x1, starting transfers between devices, body(): lax.all_to_all(gradient.astype(jnp.bfloat16), 'expert', split_axis=0, con...  10.8 us
  transfers between devices with their start and end apart: 4, of which 2 were waited for; matrix products, arithmetic and copies ran while one was open for 2% of the time, Pallas kernels for 0%

commit v1 on v0

v1 whole, which is shorter than its diff:
```python
import functools
import jax
import jax.numpy as jnp
from jax import lax
from jax.experimental import pallas as pl
from jax.experimental.pallas import tpu as pltpu
from jax.sharding import PartitionSpec as P

Q_IN = 1536
KV_IN = 512
NOPE_DIM = 128
NS_STEPS = 5
Q_OUT = 192
KV_OUT = 256

quintic_a = 3.4445
quintic_b = -4.775
quintic_c = 2.0315
norm_eps = 1e-07
beta_coef = 0.95
clip_tau = 100.0
plan_span = 10000.0
rms_match = 0.2


def split(value):
    high = value.astype(jnp.bfloat16)
    low = (value - high.astype(jnp.float32)).astype(jnp.bfloat16)
    return high, low


def dot(left, right):
    return jnp.dot(left, right, preferred_element_type=jnp.float32)


def product(left, right):
    (lh, ll), (rh, rl) = left, right
    return dot(lh, rh) + (dot(lh, rl) + dot(ll, rh))


def polar_factor(gram0):
    rows = lax.broadcasted_iota(jnp.int32, gram0.shape, 0)
    columns = lax.broadcasted_iota(jnp.int32, gram0.shape, 1)
    eye = jnp.where(rows == columns, 1.0, 0.0)
    squares = jnp.sum(jnp.sum(gram0 * eye, axis=1, keepdims=True), axis=0, keepdims=True)
    inverse = 1.0 / (jnp.sqrt(squares) + norm_eps)
    gram = (gram0 * inverse) * inverse
    factor = None
    for sweep in range(NS_STEPS):
        parts = split(gram)
        poly = quintic_a * eye + quintic_b * gram + quintic_c * product(parts, parts)
        poly_parts = split(poly)
        factor = poly if factor is None else product(split(factor), poly_parts)
        if sweep < NS_STEPS - 1:
            gram = product(split(product(parts, poly_parts)), poly_parts)
    return factor * inverse


def ns_kernel(scale_ref, rows_ref, out_ref):
    block = rows_ref[...].reshape(64, 24, KV_OUT).astype(jnp.float32)
    rows = block.reshape(Q_IN, KV_OUT).astype(jnp.bfloat16)
    gram0 = lax.dot_general(rows, rows, (((0,), (0,)), ((), ())), preferred_element_type=jnp.float32)
    factor = polar_factor(gram0) * scale_ref[pl.program_id(0)]
    high, low = split(factor)
    update = dot(rows, high) + dot(rows, low)
    out_ref[...] = update.reshape(64, 1, 24, KV_OUT).astype(jnp.bfloat16)


def newton_schulz(rows, scales):
    return pl.pallas_call(
        ns_kernel,
        grid=(2,),
        in_specs=[
            pl.BlockSpec(memory_space=pltpu.SMEM),
            pl.BlockSpec((64, 1, 24, KV_OUT), lambda i: (0, i, 0, 0)),
        ],
        out_specs=pl.BlockSpec((64, 1, 24, KV_OUT), lambda i: (0, i, 0, 0)),
        out_shape=jax.ShapeDtypeStruct((64, 2, 24, KV_OUT), jnp.bfloat16),
        compiler_params=pltpu.CompilerParams(vmem_limit_bytes=48 * 2**20),
    )(scales, rows)


def live_limits(block_kind):
    in_live = jnp.where(block_kind == 0, Q_IN, KV_IN)
    out_live = jnp.where(block_kind == 0, Q_OUT, KV_OUT)
    return (in_live, out_live)


def body(grad_parts, momentum, block_ids, step, logit_max):
    owners = lax.axis_size("expert")
    column = lax.axis_index("expert")
    slot_rows = momentum.shape[0]
    piece_rows = momentum.shape[1]
    slots_each = slot_rows // owners
    head_peaks = jnp.max(lax.all_gather(logit_max[0, 0], ("dp", "expert"), axis=0, tiled=False), axis=0)
    summed = lax.psum_scatter(
        grad_parts[0], "dp", scatter_dimension=0, tiled=True
    ).astype(jnp.float32)
    step_rate = 0.1 + 0.45 * (1.0 + jnp.cos(jnp.pi * step[0].astype(jnp.float32) / plan_span))
    block_kind = block_ids % 2
    in_live, out_live = live_limits(block_kind)
    in_pos = column * piece_rows + jnp.arange(piece_rows)
    live_mask = (in_pos[None, :, None] < in_live[:, None, None]) & (
        jnp.arange(KV_OUT)[None, None, :] < out_live[:, None, None]
    )
    gradient = jnp.where(live_mask, summed, 0.0)
    fresh = jnp.where(live_mask, beta_coef * momentum.astype(jnp.float32) + gradient, 0.0).astype(jnp.bfloat16)
    nesterov = (gradient + beta_coef * fresh.astype(jnp.float32)).astype(jnp.bfloat16)
    own_kind = lax.dynamic_slice_in_dim(block_kind, column * slots_each, slots_each, 0)
    widest = jnp.where(own_kind == 0, max(Q_IN, Q_OUT), max(KV_IN, KV_OUT))
    scales = step_rate * rms_match * jnp.sqrt(widest.astype(jnp.float32))
    own = lax.all_to_all(nesterov, "expert", split_axis=0, concat_axis=0, tiled=True)
    update_own = newton_schulz(own.reshape(owners, slots_each, piece_rows, KV_OUT), scales)
    update_rows = lax.all_to_all(
        update_own.reshape(slot_rows, piece_rows, KV_OUT), "expert", split_axis=0, concat_axis=0, tiled=True
    )
    clip_eta = jnp.minimum(1.0, clip_tau / head_peaks).reshape(-1)
    head_pair = block_ids // 2
    picker = head_pair[:, None] == jnp.arange(clip_eta.shape[0])[None, :]
    slot_eta = jnp.sum(jnp.where(picker, clip_eta[None, :], 0.0), axis=1)
    out_rows = jnp.arange(KV_OUT)[None, :]
    root_eta = jnp.sqrt(slot_eta)[:, None]
    query_rows = jnp.where(
        out_rows < NOPE_DIM, root_eta, jnp.where(out_rows < Q_OUT, slot_eta[:, None], 0.0)
    )
    value_rows = jnp.where(out_rows < NOPE_DIM, root_eta, 1.0)
    clip_scale = jnp.where((block_kind == 0)[:, None], query_rows, value_rows)
    return (fresh, update_rows, clip_scale)


def solution(mesh):
    in_specs = (
        P("dp", None, "expert", None),
        P("dp", "expert", None),
        P("dp"),
        P(),
        P("dp", "expert", None, None),
    )
    out_specs = (P("dp", "expert", None), P("dp", "expert", None), P("dp", None))
    return jax.shard_map(body, mesh=mesh, in_specs=in_specs, out_specs=out_specs, check_vma=False)
```

time: 352 us -> 259 us (0.74)
  matrix products: 48.3 us -> 0 us
  blocking collectives: 126 us -> 95.9 us
  local copies, waits for them, and re-layouts: 17.6 us -> 1.25 us
  waiting for transfers between devices: 95.8 us -> 112 us
  starting transfers between devices: 30.4 us -> 17.1 us
  Pallas kernels: 0 us -> 12.9 us
  other arithmetic: 16.1 us -> 5.19 us
    all_gather x0 -> x1, blocking collectives: none -> 95.9 us  [body(): lax.all_gather(logit_max[0, 0], ('dp', 'expert'), axis=0, tiled=False)]
    pmax x1 -> x0, blocking collectives: 81.1 us -> none  [body(): head_peaks = lax.pmax(logit_max[0, 0], ('dp', 'expert'))]
    dot_general x30 -> x0, matrix products: 48.3 us -> none  [the longest x10 27.7 us: orthogonalize(): lax.dot_general(current, current, (((0,), (0,)), ((), ())), precision=ful...]
    all_to_all x1 -> x0, blocking collectives: 45.3 us -> none  [body(): lax.all_to_all(update_own, 'expert', split_axis=1, concat_axis=0, tiled=T...]
    all_to_all x3 -> x2, starting transfers between devices: 30.4 us -> 17.1 us  [the longest x1 10.6 us: body(): lax.all_to_all(nesterov, 'expert', split_axis=0, concat_axis=0, tiled=True)]
    reduce_scatter x1, waiting for transfers between devices: 59.8 us -> 72.8 us  [body(): lax.psum_scatter(grad_parts[0], 'dp', scatter_dimension=0, tiled=True)]
    pallas_call x0 -> x1, Pallas kernels: none -> 12.9 us  [newton_schulz(): pl.pallas_call(ns_kernel, grid=(2,), in_specs=[pl.BlockSpec(memory_space=...]
    convert_element_type x2 -> x0, local copies, waits for them, and re-layouts: 12.3 us -> none  [the longest x1 9.65 us: body(): update_own = (scales[:, None, None] * orthogonal).astype(jnp.bfloat16)]
  transfers between devices with their start and end apart: 4 -> 3, of which waited for: 2 -> 2; matrix products, arithmetic and copies ran while one was open for 2% -> 1% of each run, Pallas kernels for 0% -> 0%
where the time goes in v1:
time: 259 us
  waiting for transfers between devices  112 us (43%)
  blocking collectives  95.9 us (37%)
  starting transfers between devices  17.1 us (7%)
  between operations  14.9 us (6%)
  Pallas kernels  12.9 us (5%)
  other arithmetic  5.19 us (2%)
    all_gather x1, blocking collectives, body(): lax.all_gather(logit_max[0, 0], ('dp', 'expert'), axis=0, tiled=False)  95.9 us
    reduce_scatter x1, waiting for transfers between devices, body(): lax.psum_scatter(grad_parts[0], 'dp', scatter_dimension=0, tiled=True)  72.8 us
    all_to_all x1, waiting for transfers between devices, body(): lax.all_to_all(nesterov, 'expert', split_axis=0, concat_axis=0, tiled=True)  38.2 us
    pallas_call x1, Pallas kernels, newton_schulz(): pl.pallas_call(ns_kernel, grid=(2,), in_specs=[pl.BlockSpec(memory_space=...  12.9 us
    all_to_all x1, starting transfers between devices, body(): lax.all_to_all(nesterov, 'expert', split_axis=0, concat_axis=0, tiled=True)  10.6 us
    all_to_all x1, starting transfers between devices, body(): lax.all_to_all(update_own.reshape(slot_rows, piece_rows, KV_OUT), 'expert...  6.46 us
  transfers between devices with their start and end apart: 3, of which 2 were waited for; matrix products, arithmetic and copies ran while one was open for 1% of the time, Pallas kernels for 0%

profile of v1, /device:TPU:1, one launch (start us, length us, event | category | flops | bytes accessed | tf_op | source)
XLA Modules:
  0.0 258.9 jit_solution(14187510835989646700)
XLA Ops:
  7.2 0.0 reduce-scatter.2.cloned.1.call-start
  7.2 0.0 copy-start.2
  7.2 0.0 copy-start
  7.2 0.7 reduce-scatter.2.cloned.1.call-update
  7.9 0.0 copy-done.2
  8.0 0.1 broadcast_compare_fusion
  8.0 0.1 iota_compare_fusion.1
  8.1 72.8 %reduce-scatter.2.cloned.1.call-done = bf16[128,24,256]{2,1,0:T(8,128)(2,1)} async-done(((bf16[512,24,256]{2,1,0:T(8,128)(2,1)}), bf16[128,24,256]{2,1,0:T(8,128)(2,1)}) %reduce-scatter.2.cloned.1.call-update) | async-done | bytes 1572880 | tf_op jit(solution)/shard_map/reduce_scatter | solution.py:96
  81.0 0.0 copy-done
  81.0 3.7 %add_convert_fusion = (bf16[128,24,256]{2,1,0:T(8,128)(2,1)}, bf16[128,24,256]{2,1,0:T(8,128)(2,1)}) fusion(bf16[128,24,256]{2,1,0:T(8,128)(2,1)} %reduce-scatter.2.cloned.1.call-done, pred[128,256]{1,0:T(8,128)(4,1)S(1)} %iota_compare_fusion.1, pred[128,24]{1,0:T(8,128)(4,1)S(1)} %broadcast_compare_fusion, bf16[128,24,256]{2,1,0:T(8,128)(2,1)S(1)} %copy-done), kind=kLoop, calls=%fused_computation.3 | loop fusion | flops 9437184 | bytes 6327296 | tf_op jit(solution)/shard_map/convert_element_type | solution.py:108
  84.6 10.6 %all-to-all-start = ((bf16[128,24,256]{2,1,0:T(8,128)(2,1)}), bf16[128,24,256]{2,1,0:T(8,128)(2,1)S(1)}, u32[]{:S(2)}, u32[]{:S(2)}) async-start(bf16[128,24,256]{2,1,0:T(8,128)(2,1)} %get-tuple-element.5), calls=%async_computation.1 | async-start | bytes 3145728 | tf_op jit(solution)/shard_map/all_to_all | solution.py:112
  96.0 0.1 fusion.3.scale_ref
  96.0 38.2 %all-to-all-done = bf16[128,24,256]{2,1,0:T(8,128)(2,1)S(1)} async-done(((bf16[128,24,256]{2,1,0:T(8,128)(2,1)}), bf16[128,24,256]{2,1,0:T(8,128)(2,1)S(1)}, u32[]{:S(2)}, u32[]{:S(2)}) %all-to-all-start) | async-done | bytes 1572896 | tf_op jit(solution)/shard_map/all_to_all | solution.py:112
  134.2 0.0 copy-start.1
  134.2 12.9 %shard_map.76 = bf16[64,2,24,256]{3,2,1,0:T(8,128)(2,1)} custom-call(f32[2]{0:T(128)S(1)} %fusion.3.scale_ref, bf16[64,2,24,256]{3,2,1,0:T(8,128)(2,1)S(1)} %bitcast.4), custom_call_target="tpu_custom_call" | custom-call | tf_op jit(solution)/shard_map/pallas_call | solution.py:70
  147.1 6.5 %all-to-all-start.1 = ((bf16[128,24,256]{2,1,0:T(8,128)(2,1)}), bf16[128,24,256]{2,1,0:T(8,128)(2,1)S(1)}, u32[]{:S(2)}, u32[]{:S(2)}) async-start(bf16[128,24,256]{2,1,0:T(8,128)(2,1)} %bitcast.3), calls=%async_computation.2 | async-start | bytes 3145728 | tf_op jit(solution)/shard_map/all_to_all | solution.py:114
  153.6 0.0 copy-done.1
  153.6 95.9 %all-gather = f32[256,1,4,64]{3,2,1,0:T(4,128)S(1)} all-gather(f32[1,1,4,64]{3,2,1,0:T(4,128)S(1)} %copy-done.1), channel_id=2, replica_groups=mesh['dp'=4,'expert'=64] {'dp','expert'}, dimensions={0}, use_global_device_ids=true | all-gather | bytes 263168 | tf_op jit(solution)/shard_map/all_gather | solution.py:95
  249.5 0.3 reduce_max.9
  249.8 0.1 min.15
  249.9 0.2 select_reduce_fusion
  250.1 0.8 select_select_fusion
  250.9 0.0 all-to-all-done.1
  250.9 1.1 copy.10
  (7 shorter events, 0.0 us)
Async XLA Ops:
  7.2 73.8 %reduce-scatter.2.cloned.1.call-start = ((), (), s32[]{:S(2)}) async-start(), calls=%async_computation.3 | async-start | bytes 7864320 | tf_op jit(solution)/shard_map/reduce_scatter | solution.py:96
  7.2 0.7 copy-start.2
  7.2 73.7 %copy-start = (bf16[128,24,256]{2,1,0:T(8,128)(2,1)S(1)}, bf16[128,24,256]{2,1,0:T(8,128)(2,1)}, u32[]{:S(2)}) copy-start(bf16[128,24,256]{2,1,0:T(8,128)(2,1)} %param.6) | copy-start | bytes 4718596
  84.6 49.6 %all-to-all-start = ((bf16[128,24,256]{2,1,0:T(8,128)(2,1)}), bf16[128,24,256]{2,1,0:T(8,128)(2,1)S(1)}, u32[]{:S(2)}, u32[]{:S(2)}) async-start(bf16[128,24,256]{2,1,0:T(8,128)(2,1)} %get-tuple-element.5), calls=%async_computation.1 | async-start | bytes 3145728 | tf_op jit(solution)/shard_map/all_to_all | solution.py:112
  134.2 19.3 %copy-start.1 = (f32[1,1,4,64]{3,2,1,0:T(4,128)S(1)}, f32[1,1,4,64]{3,2,1,0:T(4,128)}, u32[]{:S(2)}) copy-start(f32[1,1,4,64]{3,2,1,0:T(4,128)} %param.9) | copy-start | bytes 3076
  147.1 103.8 %all-to-all-start.1 = ((bf16[128,24,256]{2,1,0:T(8,128)(2,1)}), bf16[128,24,256]{2,1,0:T(8,128)(2,1)S(1)}, u32[]{:S(2)}, u32[]{:S(2)}) async-start(bf16[128,24,256]{2,1,0:T(8,128)(2,1)} %bitcast.3), calls=%async_computation.2 | async-start | bytes 3145728 | tf_op jit(solution)/shard_map/all_to_all | solution.py:114
Sparse Core Ops, SparseCore 0:
  10.6 70.3 reduce-scatter.1

commit v2 on v1

v2 whole, which is shorter than its diff:
```python
import math

import jax
import jax.numpy as jnp
from jax import lax
from jax.experimental import pallas as pl
from jax.experimental.pallas import tpu as pltpu
from jax.sharding import PartitionSpec as P

Q_IN = 1536
KV_IN = 512
NOPE_DIM = 128
NS_STEPS = 5
Q_OUT = 192
KV_OUT = 256
ROWS = 24
SLOTS = 128
ROUNDS = 4
PER = 32
HALF = 16
Z = 8
X = 4
DP = 4
MESH = pl.DeviceIdType.MESH

quintic_a = 3.4445
quintic_b = -4.775
quintic_c = 2.0315
norm_eps = 1e-07
beta_coef = 0.95
clip_tau = 100.0
plan_span = 10000.0
rms_match = 0.2
QUERY_SCALE = rms_match * math.sqrt(max(Q_IN, Q_OUT))
VALUE_SCALE = rms_match * math.sqrt(max(KV_IN, KV_OUT))


def split(value):
    high = value.astype(jnp.bfloat16)
    low = (value - high.astype(jnp.float32)).astype(jnp.bfloat16)
    return high, low


def dot(left, right):
    return jnp.dot(left, right, preferred_element_type=jnp.float32)


def product(left, right):
    (lh, ll), (rh, rl) = left, right
    return dot(lh, rh) + (dot(lh, rl) + dot(ll, rh))


def polar_factor(gram0):
    rows = lax.broadcasted_iota(jnp.int32, gram0.shape, 0)
    columns = lax.broadcasted_iota(jnp.int32, gram0.shape, 1)
    eye = jnp.where(rows == columns, 1.0, 0.0)
    squares = jnp.sum(jnp.sum(gram0 * eye, axis=1, keepdims=True), axis=0, keepdims=True)
    inverse = 1.0 / (jnp.sqrt(squares) + norm_eps)
    gram = (gram0 * inverse) * inverse
    factor = None
    for sweep in range(NS_STEPS):
        parts = split(gram)
        poly = quintic_a * eye + quintic_b * gram + quintic_c * product(parts, parts)
        poly_parts = split(poly)
        factor = poly if factor is None else product(split(factor), poly_parts)
        if sweep < NS_STEPS - 1:
            gram = product(split(product(parts, poly_parts)), poly_parts)
    return factor * inverse


def step_kernel(
    ids_ref, rate_ref, grads, momentum, logit, fresh_out, update_out, peaks_out,
    own, near_up, near_down, held, relay_up, relay_down, in_up, in_down, nest, fresh, owned, back,
    peak_dp, peak_row, peak_col, peak_a, peak_b,
    load_sem, relay_send, relay_sem, raw_send, sum_send, in_sem, go_send, go_sem, back_send, back_sem, fresh_sem,
    peak_send, peak_sem,
):
    d = lax.axis_index("dp")
    e = lax.axis_index("expert")
    z, x, core = e // (2 * X), (e // 2) % X, e % 2
    place = e // 2
    up, down, far = (d + 1) % DP, (d + 3) % DP, (d + 2) % DP

    def shifted(k):
        return ((z + k % Z) % Z) * X + (x + k // Z) % X

    def remote(source, target, send, recv, where):
        return pltpu.make_async_remote_copy(
            src_ref=source, dst_ref=target, send_sem=send, recv_sem=recv, device_id=where, device_id_type=MESH
        )

    def drain(ref, sem):
        pltpu.make_async_copy(ref, ref, sem).wait()

    loads = [
        pltpu.make_async_copy(grads.at[up, :, 0], near_up, load_sem.at[0]),
        pltpu.make_async_copy(grads.at[down, :, 1], near_down, load_sem.at[1]),
        pltpu.make_async_copy(grads.at[d], own, load_sem.at[2]),
        pltpu.make_async_copy(momentum, held, load_sem.at[3]),
    ]
    for load in loads:
        load.start()

    barrier = pltpu.get_barrier_semaphore()

    def greet(k, _):
        pl.semaphore_signal(barrier, inc=1, device_id=(d, (e + k) % (2 * X * Z)), device_id_type=MESH)
        return 0

    for other in (up, down, far):
        pl.semaphore_signal(barrier, inc=1, device_id=(other, e), device_id_type=MESH)
    lax.fori_loop(1, 2 * X * Z, greet, 0)
    pl.semaphore_wait(barrier, 2 * X * Z + 2)

    def relay(r):
        remote(grads.at[far, r, 0], relay_down.at[r], relay_send, relay_sem.at[r, 0], (up, e)).start()
        remote(grads.at[far, r, 1], relay_up.at[r], relay_send, relay_sem.at[r, 1], (down, e)).start()

    def raw(r):
        remote(grads.at[up, r, 1], in_down.at[r, 1], raw_send, in_sem.at[r, 0], (up, e)).start()
        remote(grads.at[down, r, 0], in_up.at[r, 0], raw_send, in_sem.at[r, 1], (down, e)).start()

    def combine(r):
        for side, (near, relayed) in enumerate(((near_up, relay_down), (near_down, relay_up))):
            drain(relayed.at[r], relay_sem.at[r, side])

            def add(i, _, near=near, relayed=relayed):
                near[r, i] = (near[r, i].astype(jnp.float32) + relayed[r, i].astype(jnp.float32)).astype(jnp.bfloat16)
                return 0

            lax.fori_loop(0, HALF, add, 0)
            if side == 0:
                remote(near_up.at[r], in_down.at[r, 0], sum_send, in_sem.at[r, 0], (up, e)).start()
            else:
                remote(near_down.at[r], in_up.at[r, 1], sum_send, in_sem.at[r, 1], (down, e)).start()

    row = e * ROWS + lax.broadcasted_iota(jnp.int32, (ROWS, KV_OUT), 0)
    column = lax.broadcasted_iota(jnp.int32, (ROWS, KV_OUT), 1)
    query_live = jnp.where(column < Q_OUT, 1.0, 0.0)
    value_live = jnp.where(row < KV_IN, 1.0, 0.0)

    def home(r):
        drain(in_down.at[r], in_sem.at[r, 0])
        drain(in_up.at[r], in_sem.at[r, 1])
        for half in range(2):

            def one(i, _, half=half):
                slot = r * PER + half * HALF + i
                query = (1 - ids_ref[slot] % 2).astype(jnp.float32)
                live = value_live + query * (query_live - value_live)
                total = own[r, half, i].astype(jnp.float32) + (
                    in_down[r, half, i].astype(jnp.float32) + in_up[r, half, i].astype(jnp.float32)
                )
                gradient = live * total
                state = (live * (beta_coef * held[slot].astype(jnp.float32) + gradient)).astype(jnp.bfloat16)
                fresh[slot] = state
                nest[slot] = (gradient + beta_coef * state.astype(jnp.float32)).astype(jnp.bfloat16)
                return 0

            lax.fori_loop(0, HALF, one, 0)
        pltpu.make_async_copy(fresh.at[pl.ds(r * PER, PER)], fresh_out.at[pl.ds(r * PER, PER)], fresh_sem).start()

    def go(r):
        def send(k, _):
            rank = shifted(k)
            target = 2 * rank + r % 2

            @pl.when(target != e)
            def _():
                remote(nest.at[r * PER + rank], owned.at[r // 2, e], go_send.at[r], go_sem.at[r // 2], (d, target)).start()

            @pl.when(target == e)
            def _():
                pltpu.make_async_copy(nest.at[r * PER + rank], owned.at[r // 2, e], go_sem.at[r // 2]).start()

            return 0

        lax.fori_loop(0, PER, send, 0)

    def orthogonalize(j):
        slot = (2 * j + core) * PER + place
        query = (1 - ids_ref[slot] % 2).astype(jnp.float32)
        width = VALUE_SCALE + query * (QUERY_SCALE - VALUE_SCALE)
        drain(owned.at[j], go_sem.at[j])
        block = owned[j].astype(jnp.float32)
        rows = block.reshape(Q_IN, KV_OUT).astype(jnp.bfloat16)
        gram0 = lax.dot_general(rows, rows, (((0,), (0,)), ((), ())), preferred_element_type=jnp.float32)
        factor = polar_factor(gram0) * (width * rate_ref[0])
        high, low = split(factor)
        update = dot(rows, high) + dot(rows, low)
        back[j] = update.reshape(2 * X * Z, ROWS, KV_OUT).astype(jnp.bfloat16)

    def give(j):
        slot = (2 * j + core) * PER + place

        def send(k, _):
            target = 2 * shifted(k // 2) + (core + k % 2) % 2

            @pl.when(target != e)
            def _():
                remote(back.at[j, target], update_out.at[slot], back_send.at[j], back_sem, (d, target)).start()

            @pl.when(target == e)
            def _():
                pltpu.make_async_copy(back.at[j, target], update_out.at[slot], back_sem).start()

            return 0

        lax.fori_loop(0, 2 * X * Z, send, 0)

    for source, side in ((up, 0), (down, 0), (far, 0)):
        remote(logit, peak_dp.at[d], peak_send.at[0], peak_sem.at[0], (source, e)).start()
    pltpu.make_async_copy(logit, peak_dp.at[d], peak_sem.at[0]).start()

    def peaks_row():
        drain(peak_dp, peak_sem.at[0])
        peak_a[...] = jnp.max(peak_dp[...], axis=0)
        inner = 2 * x + core

        def send(k, _):
            remote(peak_a, peak_row.at[inner], peak_send.at[1], peak_sem.at[1], (d, 2 * X * z + (inner + k) % (2 * X))).start()
            return 0

        lax.fori_loop(1, 2 * X, send, 0)
        pltpu.make_async_copy(peak_a, peak_row.at[inner], peak_sem.at[1]).start()

    def peaks_column():
        drain(peak_row, peak_sem.at[1])
        peak_b[...] = jnp.max(peak_row[...], axis=0)

        def send(k, _):
            remote(peak_b, peak_col.at[z], peak_send.at[2], peak_sem.at[2], (d, 2 * X * ((z + k) % Z) + 2 * x + core)).start()
            return 0

        lax.fori_loop(1, Z, send, 0)
        pltpu.make_async_copy(peak_b, peak_col.at[z], peak_sem.at[2]).start()

    relay(0)
    raw(0)
    relay(1)
    raw(1)
    for load in loads:
        load.wait()
    combine(0)
    relay(2)
    raw(2)
    combine(1)
    relay(3)
    raw(3)
    home(0)
    go(0)
    combine(2)
    peaks_row()
    home(1)
    go(1)
    combine(3)
    peaks_column()
    home(2)
    go(2)
    orthogonalize(0)
    give(0)
    home(3)
    go(3)
    orthogonalize(1)
    give(1)

    drain(peak_col, peak_sem.at[2])
    peaks_out[...] = jnp.max(peak_col[...], axis=0)
    drain(peak_dp.at[pl.ds(0, DP - 1)], peak_send.at[0])
    drain(peak_row.at[pl.ds(0, 2 * X - 1)], peak_send.at[1])
    drain(peak_col.at[pl.ds(0, Z - 1)], peak_send.at[2])
    for sem in (relay_send, raw_send, sum_send, fresh_sem):
        drain(fresh, sem)
    for r in range(ROUNDS):

        @pl.when(core == r % 2)
        def _():
            drain(nest.at[pl.ds(0, PER - 1)], go_send.at[r])

        @pl.when(core != r % 2)
        def _():
            drain(nest.at[pl.ds(0, PER)], go_send.at[r])

    for j in range(2):
        drain(back.at[j, pl.ds(0, 2 * X * Z - 1)], back_send.at[j])
    drain(update_out, back_sem)


def fused_step(ids, rate, grads, momentum, logit):
    slab = (ROWS, KV_OUT)
    bf16 = jnp.bfloat16
    halves = pltpu.VMEM((ROUNDS, HALF) + slab, bf16)
    wholes = pltpu.VMEM((ROUNDS, 2, HALF) + slab, bf16)
    slots = pltpu.VMEM((SLOTS,) + slab, bf16)
    pair = pltpu.VMEM((2, 2 * X * Z) + slab, bf16)
    heads = logit.shape
    dma = pltpu.SemaphoreType.DMA
    smem = pl.BlockSpec(memory_space=pltpu.SMEM)
    vmem = pl.BlockSpec(memory_space=pltpu.VMEM)
    anywhere = pl.BlockSpec(memory_space=pl.ANY)
    return pl.pallas_call(
        step_kernel,
        in_specs=[smem, smem, anywhere, anywhere, vmem],
        out_specs=[anywhere, anywhere, vmem],
        out_shape=[
            jax.ShapeDtypeStruct((SLOTS,) + slab, bf16),
            jax.ShapeDtypeStruct((SLOTS,) + slab, bf16),
            jax.ShapeDtypeStruct(heads, jnp.float32),
        ],
        scratch_shapes=[
            wholes, halves, halves, slots, halves, halves, wholes, wholes, slots, slots, pair, pair,
            pltpu.VMEM((DP,) + heads, jnp.float32),
            pltpu.VMEM((2 * X,) + heads, jnp.float32),
            pltpu.VMEM((Z,) + heads, jnp.float32),
            pltpu.VMEM(heads, jnp.float32),
            pltpu.VMEM(heads, jnp.float32),
            dma((4,)), dma, dma((ROUNDS, 2)), dma, dma, dma((ROUNDS, 2)), dma((ROUNDS,)), dma((2,)), dma((2,)), dma, dma,
            dma((3,)), dma((3,)),
        ],
        compiler_params=pltpu.CompilerParams(
            collective_id=0, has_side_effects=True, vmem_limit_bytes=56 * 2**20
        ),
    )(ids, rate, grads, momentum, logit)


def body(grad_parts, momentum, block_ids, step, logit_max):
    step_rate = 0.1 + 0.45 * (1.0 + jnp.cos(jnp.pi * step.astype(jnp.float32) / plan_span))
    grads = grad_parts.reshape(DP, ROUNDS, 2, HALF, ROWS, KV_OUT)
    fresh, update_rows, head_peaks = fused_step(block_ids, step_rate, grads, momentum, logit_max[0, 0])
    clip_eta = jnp.minimum(1.0, clip_tau / head_peaks).reshape(-1)
    block_kind = block_ids % 2
    head_pair = block_ids // 2
    picker = head_pair[:, None] == jnp.arange(clip_eta.shape[0])[None, :]
    slot_eta = jnp.sum(jnp.where(picker, clip_eta[None, :], 0.0), axis=1)
    out_rows = jnp.arange(KV_OUT)[None, :]
    root_eta = jnp.sqrt(slot_eta)[:, None]
    query_rows = jnp.where(
        out_rows < NOPE_DIM, root_eta, jnp.where(out_rows < Q_OUT, slot_eta[:, None], 0.0)
    )
    value_rows = jnp.where(out_rows < NOPE_DIM, root_eta, 1.0)
    clip_scale = jnp.where((block_kind == 0)[:, None], query_rows, value_rows)
    return (fresh, update_rows, clip_scale)


def solution(mesh):
    in_specs = (
        P("dp", None, "expert", None),
        P("dp", "expert", None),
        P("dp"),
        P(),
        P("dp", "expert", None, None),
    )
    out_specs = (P("dp", "expert", None), P("dp", "expert", None), P("dp", None))
    return jax.shard_map(body, mesh=mesh, in_specs=in_specs, out_specs=out_specs, check_vma=False)
```

time: 259 us -> 126 us (0.49)
  waiting for transfers between devices: 112 us -> 0 us
  Pallas kernels: 12.9 us -> 119 us
  blocking collectives: 95.9 us -> 0 us
  starting transfers between devices: 17.1 us -> 0 us
  between operations: 14.9 us -> 1.41 us
  other arithmetic: 5.19 us -> 1.67 us
  local copies, waits for them, and re-layouts: 1.25 us -> 4.01 us
    pallas_call x1, Pallas kernels: 12.9 us -> 119 us  [fused_step(): pl.pallas_call(step_kernel, in_specs=[smem, smem, anywhere, anywhere, vme...]
    all_gather x1 -> x0, blocking collectives: 95.9 us -> none  [body(): lax.all_gather(logit_max[0, 0], ('dp', 'expert'), axis=0, tiled=False)]
    reduce_scatter x1 -> x0, waiting for transfers between devices: 72.8 us -> none  [body(): lax.psum_scatter(grad_parts[0], 'dp', scatter_dimension=0, tiled=True)]
    all_to_all x2 -> x0, waiting for transfers between devices: 38.2 us -> none  [the longest x1 38.2 us: body(): lax.all_to_all(nesterov, 'expert', split_axis=0, concat_axis=0, tiled=True)]
    all_to_all x2 -> x0, starting transfers between devices: 17.1 us -> none  [the longest x1 10.6 us: body(): lax.all_to_all(nesterov, 'expert', split_axis=0, concat_axis=0, tiled=True)]
    convert_element_type x1 -> x0, other arithmetic: 3.66 us -> none  [body(): (gradient + beta_coef * fresh.astype(jnp.float32)).astype(jnp.bfloat16)]
    unnamed x7 -> x6, local copies, waits for them, and re-layouts: 1.16 us -> 3.92 us
  transfers between devices with their start and end apart: 3 -> 0, of which waited for: 2 -> 0; matrix products, arithmetic and copies ran while one was open for 1% -> 0% of each run, Pallas kernels for 0% -> 0%
where the time goes in v2:
time: 126 us
  Pallas kernels  119 us (94%)
  local copies, waits for them, and re-layouts  4.01 us (3%)
  other arithmetic  1.67 us (1%)
  between operations  1.41 us (1%)
    pallas_call x1, Pallas kernels, fused_step(): pl.pallas_call(step_kernel, in_specs=[smem, smem, anywhere, anywhere, vme...  119 us
    unnamed x6, local copies, waits for them, and re-layouts  3.92 us

profile of v2, /device:TPU:1, one launch (start us, length us, event | category | flops | bytes accessed | tf_op | source)
XLA Modules:
  0.0 126.3 jit_solution(14871153157085273837)
XLA Ops:
  1.4 0.0 copy-start.1
  1.4 119.2 %shard_map.76 = (bf16[128,24,256]{2,1,0:T(8,128)(2,1)}, bf16[128,24,256]{2,1,0:T(8,128)(2,1)}, f32[4,64]{1,0:T(4,128)}) custom-call(s32[128]{0:T(128)} %ids_ref.1, f32[1]{0:T(128)S(6)} %add.14.rate_ref, bf16[4,4,2,16,24,256]{5,4,3,2,1,0:T(8,128)(2,1)} %bitcast.2, bf16[128,24,256]{2,1,0:T(8,128)(2,1)} %momentum.1, f32[4,64]{1,0:T(4,128)} %bitcast.3), custom_call_target="tpu_custom_call" | custom-call | tf_op jit(solution)/shard_map/pallas_call | solution.py:301
  120.6 0.7 divide_minimum_fusion
  121.2 0.1 broadcast_in_dim.75
  121.3 0.0 copy-done.1
  121.3 0.2 select_reduce_fusion
  121.6 0.8 select_select_fusion
  122.3 0.0 copy-start
  122.3 2.8 %copy.11 = bf16[128,24,256]{2,1,0:T(8,128)(2,1)} copy(bf16[128,24,256]{2,1,0:T(8,128)(2,1)} %get-tuple-element.14) | data formatting | bytes 3145728
  125.1 0.0 copy-done
  125.1 1.1 copy.12
  (4 shorter events, 0.0 us)
Async XLA Ops:
  1.4 120.0 %copy-start.1 = (s32[128]{0:T(128)S(1)}, s32[128]{0:T(128)}, u32[]{:S(2)}) copy-start(s32[128]{0:T(128)} %ids_ref.1) | copy-start | bytes 1540
  122.3 2.8 %copy-start = (bf16[128,24,256]{2,1,0:T(8,128)(2,1)S(1)}, bf16[128,24,256]{2,1,0:T(8,128)(2,1)}, u32[]{:S(2)}) copy-start(bf16[128,24,256]{2,1,0:T(8,128)(2,1)} %get-tuple-element.15) | copy-start | bytes 4718596

commit v3 on v2

v3 whole, which is shorter than its diff:
```python
import math

import jax
import jax.numpy as jnp
from jax import lax
from jax.experimental import pallas as pl
from jax.experimental.pallas import tpu as pltpu
from jax.sharding import PartitionSpec as P

Q_IN = 1536
KV_IN = 512
NOPE_DIM = 128
NS_STEPS = 5
Q_OUT = 192
KV_OUT = 256
ROWS = 24
SLOTS = 128
ROUNDS = 8
PER = 16
HALF = 8
LAG = 2
PACE = 12
Z = 8
X = 4
DP = 4
MESH = pl.DeviceIdType.MESH

quintic_a = 3.4445
quintic_b = -4.775
quintic_c = 2.0315
norm_eps = 1e-07
beta_coef = 0.95
clip_tau = 100.0
plan_span = 10000.0
rms_match = 0.2
QUERY_SCALE = rms_match * math.sqrt(max(Q_IN, Q_OUT))
VALUE_SCALE = rms_match * math.sqrt(max(KV_IN, KV_OUT))


def split(value):
    high = value.astype(jnp.bfloat16)
    low = (value - high.astype(jnp.float32)).astype(jnp.bfloat16)
    return high, low


def dot(left, right):
    return jnp.dot(left, right, preferred_element_type=jnp.float32)


def product(left, right):
    (lh, ll), (rh, rl) = left, right
    return dot(lh, rh) + (dot(lh, rl) + dot(ll, rh))


def polar_factor(gram0):
    rows = lax.broadcasted_iota(jnp.int32, gram0.shape, 0)
    columns = lax.broadcasted_iota(jnp.int32, gram0.shape, 1)
    eye = jnp.where(rows == columns, 1.0, 0.0)
    squares = jnp.sum(jnp.sum(gram0 * eye, axis=1, keepdims=True), axis=0, keepdims=True)
    inverse = 1.0 / (jnp.sqrt(squares) + norm_eps)
    gram = (gram0 * inverse) * inverse
    factor = None
    for sweep in range(NS_STEPS):
        parts = split(gram)
        poly = quintic_a * eye + quintic_b * gram + quintic_c * product(parts, parts)
        poly_parts = split(poly)
        factor = poly if factor is None else product(split(factor), poly_parts)
        if sweep < NS_STEPS - 1:
            gram = product(split(product(parts, poly_parts)), poly_parts)
    return factor * inverse


def drain(ref, sem):
    pltpu.make_async_copy(ref, ref, sem).wait()


def step_kernel(
    ids_hbm, step_ref, grads, momentum, logit_hbm, fresh, update, peaks_out,
    ids_ref, logit,
    own, near_up, near_down, held, relay_up, relay_down, in_up, in_down, nest, owned, back,
    peak_row, peak_col, peak_dp, peak_a, peak_b,
    load_sem, relay_send, relay_sem, raw_send, sum_send, in_sem, go_send, go_sem, back_send, back_sem,
    peak_send, peak_sem,
):
    d = lax.axis_index("dp")
    e = lax.axis_index("expert")
    z, x, core = e // (2 * X), (e // 2) % X, e % 2
    inner = e % (2 * X)
    family = 2 * ((x + z) % 2) + core
    place = 2 * z + x // 2
    up, down, far = (d + 1) % DP, (d + 3) % DP, (d + 2) % DP

    def remote(source, target, send, recv, where):
        return pltpu.make_async_remote_copy(
            src_ref=source, dst_ref=target, send_sem=send, recv_sem=recv, device_id=where, device_id_type=MESH
        )

    def row_peer(k):
        return 2 * X * z + (inner + k) % (2 * X)

    def column_peer(k):
        return 2 * X * ((z + k) % Z) + inner

    barrier = pltpu.get_barrier_semaphore()

    def greet(where):
        pl.semaphore_signal(barrier, inc=1, device_id=where, device_id_type=MESH)

    for other in (up, down, far):
        greet((other, e))
    for k in range(1, 2 * X):
        greet((d, row_peer(k)))
    for k in range(1, Z):
        greet((d, column_peer(k)))
    loads = [
        pltpu.make_async_copy(grads.at[up, :, 0], near_up, load_sem.at[0]),
        pltpu.make_async_copy(grads.at[down, :, 1], near_down, load_sem.at[1]),
        pltpu.make_async_copy(grads.at[d], own, load_sem.at[2]),
        pltpu.make_async_copy(momentum, held, load_sem.at[3]),
        pltpu.make_async_copy(ids_hbm, ids_ref, load_sem.at[4]),
    ]
    load_logit = pltpu.make_async_copy(logit_hbm, logit, load_sem.at[5])
    load_logit.start()
    for load in loads:
        load.start()
    pl.semaphore_wait(barrier, DP - 1 + 2 * X - 1 + Z - 1)

    def relay(r):
        remote(grads.at[far, r, 0], relay_down.at[r], relay_send, relay_sem.at[r, 0], (up, e)).start()
        remote(grads.at[far, r, 1], relay_up.at[r], relay_send, relay_sem.at[r, 1], (down, e)).start()

    def raw(r):
        remote(grads.at[up, r, 1], in_down.at[r, 1], raw_send, in_sem.at[r, 0], (up, e)).start()
        remote(grads.at[down, r, 0], in_up.at[r, 0], raw_send, in_sem.at[r, 1], (down, e)).start()

    def combine(r):
        for side, (near, relayed) in enumerate(((near_up, relay_down), (near_down, relay_up))):
            drain(relayed.at[r], relay_sem.at[r, side])

            def add(i, _, near=near, relayed=relayed):
                near[r, i] = (near[r, i].astype(jnp.float32) + relayed[r, i].astype(jnp.float32)).astype(jnp.bfloat16)
                return 0

            lax.fori_loop(0, HALF, add, 0, unroll=True)
            if side == 0:
                remote(near_up.at[r], in_down.at[r, 0], sum_send, in_sem.at[r, 0], (up, e)).start()
            else:
                remote(near_down.at[r], in_up.at[r, 1], sum_send, in_sem.at[r, 1], (down, e)).start()

    row = e * ROWS + lax.broadcasted_iota(jnp.int32, (ROWS, KV_OUT), 0)
    column = lax.broadcasted_iota(jnp.int32, (ROWS, KV_OUT), 1)
    query_live = jnp.where(column < Q_OUT, 1.0, 0.0)
    value_live = jnp.where(row < KV_IN, 1.0, 0.0)

    def home(r):
        drain(in_down.at[r], in_sem.at[r, 0])
        drain(in_up.at[r], in_sem.at[r, 1])
        for half in range(2):

            def one(i, _, half=half):
                slot = r * PER + half * HALF + i
                query = (1 - ids_ref[slot] % 2).astype(jnp.float32)
                live = value_live + query * (query_live - value_live)
                total = own[r, half, i].astype(jnp.float32) + (
                    in_down[r, half, i].astype(jnp.float32) + in_up[r, half, i].astype(jnp.float32)
                )
                gradient = live * total
                state = (live * (beta_coef * held[slot].astype(jnp.float32) + gradient)).astype(jnp.bfloat16)
                fresh[slot] = state
                nest[slot] = (gradient + beta_coef * state.astype(jnp.float32)).astype(jnp.bfloat16)
                return 0

            lax.fori_loop(0, HALF, one, 0, unroll=True)

    def go(r):
        owner = r % 4
        source = nest.at[pl.ds(r * PER, PER)]

        def route(k):
            to_z = (z + k % Z) % Z
            to_half = (x // 2 + k // Z) % 2
            target = 2 * (X * to_z + 2 * to_half + (owner // 2 + to_z) % 2) + owner % 2
            return source.at[2 * to_z + to_half], target

        def send(k, _):
            slab, target = route(k)
            remote(slab, owned.at[r // 4, e], go_send, go_sem.at[r // 4], (d, target)).start()
            return 0

        lax.fori_loop(1, PER, send, 0)

        @pl.when(owner == family)
        def _():
            pltpu.make_async_copy(source.at[place], owned.at[r // 4, e], go_sem.at[r // 4]).start()

        @pl.when(owner != family)
        def _():
            send(0, 0)

    def orthogonalize(r):
        j = r // 4
        query = (1 - ids_ref[r * PER + place] % 2).astype(jnp.float32)
        width = VALUE_SCALE + query * (QUERY_SCALE - VALUE_SCALE)
        drain(owned.at[j], go_sem.at[j])
        block = owned[j].astype(jnp.float32)
        rows = block.reshape(Q_IN, KV_OUT).astype(jnp.bfloat16)
        gram0 = lax.dot_general(rows, rows, (((0,), (0,)), ((), ())), preferred_element_type=jnp.float32)
        factor = polar_factor(gram0) * (width * step_rate)
        high, low = split(factor)
        result = dot(rows, high) + dot(rows, low)
        back[j] = result.reshape(2 * X * Z, ROWS, KV_OUT).astype(jnp.bfloat16)

    def give(j, first, last):
        slot = (4 * j + family) * PER + place

        def send(k, _):
            target = 2 * X * ((z + k % Z) % Z) + (inner + k // Z) % (2 * X)
            remote(back.at[j, target], update.at[slot], back_send, back_sem, (d, target)).start()
            return 0

        lax.fori_loop(first, last, send, 0)

    def given(t, start):
        paced = jnp.minimum(jnp.maximum(1 + (t - start + 1) * PACE, 1), 2 * X * Z)
        return jnp.where(t < ROUNDS, paced, jnp.where(t < start, 1, 2 * X * Z))

    def finish(t):
        r = t - LAG

        @pl.when(r % 4 == family)
        def _():
            orthogonalize(r)
            pltpu.make_async_copy(back.at[r // 4, e], update.at[r * PER + place], back_sem).start()

        for j in range(2):
            start = LAG + 4 * j + family
            give(j, given(t - 1, start), given(t, start))

    relay(0)
    relay(1)
    raw(0)
    load_logit.wait()
    for k in range(1, 2 * X):
        remote(logit, peak_row.at[inner], peak_send.at[0], peak_sem.at[0], (d, row_peer(k))).start()
    pltpu.make_async_copy(logit, peak_row.at[inner], peak_sem.at[0]).start()
    for load in loads:
        load.wait()
    angle = jnp.full((1, KV_OUT), step_ref[0], jnp.int32).astype(jnp.float32) * (math.pi / plan_span)
    step_rate = 0.1 + 0.45 * (1.0 + jnp.cos(angle))
    combine(0)
    raw(1)
    relay(2)
    drain(peak_row, peak_sem.at[0])
    peak_a[...] = jnp.max(peak_row[...], axis=0)
    for k in range(1, Z):
        remote(peak_a, peak_col.at[z], peak_send.at[1], peak_sem.at[1], (d, column_peer(k))).start()
    pltpu.make_async_copy(peak_a, peak_col.at[z], peak_sem.at[1]).start()

    for t in range(LAG):
        combine(t + 1)
        raw(t + 2)
        relay(t + 3)
        home(t)
        if t == 0:
            drain(peak_col, peak_sem.at[1])
            peak_b[...] = jnp.max(peak_col[...], axis=0)
            for other in (up, down, far):
                remote(peak_b, peak_dp.at[d], peak_send.at[2], peak_sem.at[2], (other, e)).start()
            pltpu.make_async_copy(peak_b, peak_dp.at[d], peak_sem.at[2]).start()
        go(t)

    def step(t, _):
        @pl.when(t + 1 < ROUNDS)
        def _():
            combine(t + 1)

        @pl.when(t + 2 < ROUNDS)
        def _():
            raw(t + 2)

        @pl.when(t + 3 < ROUNDS)
        def _():
            relay(t + 3)

        @pl.when(t < ROUNDS)
        def _():
            home(t)
            go(t)

        finish(t)
        return 0

    lax.fori_loop(LAG, ROUNDS + LAG, step, 0)

    drain(peak_dp, peak_sem.at[2])
    peaks_out[...] = jnp.max(peak_dp[...], axis=0)
    drain(peak_row.at[pl.ds(0, 2 * X - 1)], peak_send.at[0])
    drain(peak_col.at[pl.ds(0, Z - 1)], peak_send.at[1])
    drain(peak_dp.at[pl.ds(0, DP - 1)], peak_send.at[2])
    for sem in (relay_send, raw_send, sum_send):
        drain(nest, sem)
    drain(nest.at[pl.ds(0, SLOTS - 2)], go_send)
    drain(nest.at[pl.ds(0, SLOTS - 2)], back_send)
    drain(update, back_sem)


def fused_step(ids, step, grads, momentum, logit):
    slab = (ROWS, KV_OUT)
    bf16 = jnp.bfloat16
    halves = pltpu.VMEM((ROUNDS, HALF) + slab, bf16)
    wholes = pltpu.VMEM((ROUNDS, 2, HALF) + slab, bf16)
    slots = pltpu.VMEM((SLOTS,) + slab, bf16)
    pair = pltpu.VMEM((2, 2 * X * Z) + slab, bf16)
    heads = logit.shape
    dma = pltpu.SemaphoreType.DMA
    vmem = pl.BlockSpec(memory_space=pltpu.VMEM)
    hbm = pl.BlockSpec(memory_space=pltpu.HBM)
    return pl.pallas_call(
        step_kernel,
        in_specs=[hbm, pl.BlockSpec(memory_space=pltpu.SMEM), hbm, hbm, hbm],
        out_specs=[vmem, vmem, vmem],
        out_shape=[
            pltpu.VMEM((SLOTS,) + slab, bf16),
            pltpu.VMEM((SLOTS,) + slab, bf16),
            pltpu.VMEM(heads, jnp.float32),
        ],
        scratch_shapes=[
            pltpu.SMEM(ids.shape, jnp.int32),
            pltpu.VMEM(heads, jnp.float32),
            wholes, halves, halves, slots, halves, halves, wholes, wholes, slots, pair, pair,
            pltpu.VMEM((2 * X,) + heads, jnp.float32),
            pltpu.VMEM((Z,) + heads, jnp.float32),
            pltpu.VMEM((DP,) + heads, jnp.float32),
            pltpu.VMEM(heads, jnp.float32),
            pltpu.VMEM(heads, jnp.float32),
            dma((6,)), dma, dma((ROUNDS, 2)), dma, dma, dma((ROUNDS, 2)), dma, dma((2,)), dma, dma,
            dma((3,)), dma((3,)),
        ],
        compiler_params=pltpu.CompilerParams(
            collective_id=0, has_side_effects=True, vmem_limit_bytes=40 * 2**20
        ),
    )(ids, step, grads, momentum, logit)


def tail_kernel(ids_ref, peaks_ref, fresh, update, fresh_out, update_out, clip_ref, sems):
    copies = [
        pltpu.make_async_copy(fresh, fresh_out, sems.at[0]),
        pltpu.make_async_copy(update, update_out, sems.at[1]),
    ]
    for copy in copies:
        copy.start()
    eta = jnp.minimum(1.0, clip_tau / peaks_ref[...])
    ids = jnp.transpose(jnp.broadcast_to(ids_ref[...], (SLOTS, SLOTS)))[:, 0:1]
    kind = ids % 2
    layer = ids // (2 * eta.shape[1])
    head = (ids // 2) % eta.shape[1]
    lanes = lax.broadcasted_iota(jnp.int32, (SLOTS, eta.shape[1]), 1)
    picked = jnp.zeros((SLOTS, eta.shape[1]), jnp.float32)
    for level in range(eta.shape[0]):
        picked = jnp.where(layer == level, eta[level : level + 1, :], picked)
    slot_eta = jnp.sum(jnp.where(lanes == head, picked, 0.0), axis=1, keepdims=True)
    column = lax.broadcasted_iota(jnp.int32, (SLOTS, KV_OUT), 1)
    rest = jnp.where(kind == 0, jnp.where(column < Q_OUT, slot_eta, 0.0), 1.0)
    clip_ref[...] = jnp.where(column < NOPE_DIM, jnp.sqrt(slot_eta), rest)
    for copy in copies:
        copy.wait()


def write_out(ids, peaks, fresh, update):
    vmem = pl.BlockSpec(memory_space=pltpu.VMEM)
    anywhere = pl.BlockSpec(memory_space=pl.ANY)
    return pl.pallas_call(
        tail_kernel,
        in_specs=[vmem, vmem, vmem, vmem],
        out_specs=[anywhere, anywhere, vmem],
        out_shape=[
            jax.ShapeDtypeStruct(fresh.shape, fresh.dtype),
            jax.ShapeDtypeStruct(update.shape, update.dtype),
            jax.ShapeDtypeStruct((SLOTS, KV_OUT), jnp.float32),
        ],
        scratch_shapes=[pltpu.SemaphoreType.DMA((2,))],
    )(ids, peaks, fresh, update)


def body(grad_parts, momentum, block_ids, step, logit_max):
    grads = grad_parts.reshape(DP, ROUNDS, 2, HALF, ROWS, KV_OUT)
    ids, grads, momentum, logit = (
        pltpu.with_memory_space_constraint(a, pltpu.HBM) for a in (block_ids, grads, momentum, logit_max[0, 0])
    )
    results = fused_step(ids, step, grads, momentum, logit)
    fresh, update, peaks = (pltpu.with_memory_space_constraint(a, pltpu.VMEM) for a in results)
    return tuple(write_out(block_ids.reshape(1, SLOTS), peaks, fresh, update))


def solution(mesh):
    in_specs = (
        P("dp", None, "expert", None),
        P("dp", "expert", None),
        P("dp"),
        P(),
        P("dp", "expert", None, None),
    )
    out_specs = (P("dp", "expert", None), P("dp", "expert", None), P("dp", None))
    return jax.shard_map(body, mesh=mesh, in_specs=in_specs, out_specs=out_specs, check_vma=False)
```

time: 126 us -> 105 us (0.83)
  Pallas kernels: 119 us -> 104 us
  local copies, waits for them, and re-layouts: 4.01 us -> 0 us
  other arithmetic: 1.67 us -> 0 us
    pallas_call x1 -> x2, Pallas kernels: 119 us -> 104 us  [the longest x1 101 us: fused_step(): pl.pallas_call(step_kernel, in_specs=[hbm, pl.BlockSpec(memory_space=pltp...]
    unnamed x6 -> x0, local copies, waits for them, and re-layouts: 3.92 us -> none
where the time goes in v3:
time: 105 us
  Pallas kernels  104 us (99%)
  between operations  1.28 us (1%)
    pallas_call x1, Pallas kernels, fused_step(): pl.pallas_call(step_kernel, in_specs=[hbm, pl.BlockSpec(memory_space=pltp...  101 us
    pallas_call x1, Pallas kernels, write_out(): pl.pallas_call(tail_kernel, in_specs=[vmem, vmem, vmem, vmem], out_specs=...  2.99 us

profile of v3, /device:TPU:1, one launch (start us, length us, event | category | flops | bytes accessed | tf_op | source)
XLA Modules:
  0.0 105.2 jit_solution(1017962011696265219)
XLA Ops:
  1.3 100.9 %shard_map.76 = (bf16[128,24,256]{2,1,0:T(8,128)(2,1)S(1)}, bf16[128,24,256]{2,1,0:T(8,128)(2,1)S(1)}, f32[4,64]{1,0:T(4,128)S(1)}) custom-call(s32[128]{0:T(128)} %ids_hbm.1, s32[1]{0:T(128)S(6)} %copy.8.step_ref, bf16[4,8,2,8,24,256]{5,4,3,2,1,0:T(8,128)(2,1)} %bitcast.3, bf16[128,24,256]{2,1,0:T(8,128)(2,1)} %momentum.1, f32[4,64]{1,0:T(4,128)} %bitcast.4), custom_call_target="tpu_custom_call" | custom-call | tf_op jit(solution)/shard_map/pallas_call | solution.py:318
  102.2 3.0 %shard_map.77 = (bf16[128,24,256]{2,1,0:T(8,128)(2,1)}, bf16[128,24,256]{2,1,0:T(8,128)(2,1)}, f32[128,256]{1,0:T(8,128)}) custom-call(s32[1,128]{1,0:T(1,128)} %bitcast.5, f32[4,64]{1,0:T(4,128)S(1)} %get-tuple-element.6.peaks_ref, bf16[128,24,256]{2,1,0:T(8,128)(2,1)S(1)} %get-tuple-element.7.fresh, bf16[128,24,256]{2,1,0:T(8,128)(2,1)S(1)} %get-tuple-element.8.update), custom_call_target="tpu_custom_call" | custom-call | tf_op jit(solution)/shard_map/pallas_call | solution.py:372

commit v4 on v3

--- a/solution.py
+++ b/solution.py
@@ -19,10 +19,14 @@
 PER = 16
 HALF = 8
 LAG = 2
-PACE = 12
+PACE = 16
 Z = 8
 X = 4
 DP = 4
+FULL = -(-KV_IN // ROWS)
+ALL = 6
+FEW = 5
+ARRIVING = FULL * ALL + (2 * X * Z - FULL) * FEW
 MESH = pl.DeviceIdType.MESH
 
 quintic_a = 3.4445
@@ -77,7 +81,7 @@
 def step_kernel(
     ids_hbm, step_ref, grads, momentum, logit_hbm, fresh, update, peaks_out,
     ids_ref, logit,
-    own, near_up, near_down, held, relay_up, relay_down, in_up, in_down, nest, owned, back,
+    own, near_up, near_down, held, relay_up, relay_down, in_up, in_down, nest, owned, back, returned,
     peak_row, peak_col, peak_dp, peak_a, peak_b,
     load_sem, relay_send, relay_sem, raw_send, sum_send, in_sem, go_send, go_sem, back_send, back_sem,
     peak_send, peak_sem,
@@ -151,6 +155,19 @@
     column = lax.broadcasted_iota(jnp.int32, (ROWS, KV_OUT), 1)
     query_live = jnp.where(column < Q_OUT, 1.0, 0.0)
     value_live = jnp.where(row < KV_IN, 1.0, 0.0)
+    lane = lax.broadcasted_iota(jnp.int32, (8, 128), 1)
+    wide = e < FULL
+    wide_tile = 0 * lane + e < FULL
+
+    def by_width(act):
+        @pl.when(wide)
+        def _():
+            act(ALL)
+
+        @pl.when(jnp.logical_not(wide))
+        def _():
+            act(FEW)
+
 
     def home(r):
         drain(in_down.at[r], in_sem.at[r, 0])
@@ -167,58 +184,141 @@
                 gradient = live * total
                 state = (live * (beta_coef * held[slot].astype(jnp.float32) + gradient)).astype(jnp.bfloat16)
                 fresh[slot] = state
-                nest[slot] = (gradient + beta_coef * state.astype(jnp.float32)).astype(jnp.bfloat16)
+                ahead = gradient + beta_coef * state.astype(jnp.float32)
+                left = ahead[:, :128].reshape(3, 8, 128)
+                right = ahead[:, 128:].reshape(3, 8, 128)
+                folded = jnp.where(wide_tile, right[0], right[0] + pltpu.roll(right[1], 64, 1))
+                second = jnp.where(wide_tile, right[1], right[2])
+                tiles = jnp.concatenate([left, folded[None], second[None], right[2:3]], axis=0)
+                nest[slot] = tiles.astype(jnp.bfloat16)
                 return 0
 
             lax.fori_loop(0, HALF, one, 0, unroll=True)
 
     def go(r):
         owner = r % 4
-        source = nest.at[pl.ds(r * PER, PER)]
+        first = (r // 4) * 2 * X * Z * ALL + e * ALL
 
         def route(k):
             to_z = (z + k % Z) % Z
             to_half = (x // 2 + k // Z) % 2
             target = 2 * (X * to_z + 2 * to_half + (owner // 2 + to_z) % 2) + owner % 2
-            return source.at[2 * to_z + to_half], target
-
-        def send(k, _):
-            slab, target = route(k)
-            remote(slab, owned.at[r // 4, e], go_send, go_sem.at[r // 4], (d, target)).start()
-            return 0
-
-        lax.fori_loop(1, PER, send, 0)
-
-        @pl.when(owner == family)
-        def _():
-            pltpu.make_async_copy(source.at[place], owned.at[r // 4, e], go_sem.at[r // 4]).start()
-
-        @pl.when(owner != family)
-        def _():
-            send(0, 0)
+            return r * PER + 2 * to_z + to_half, target
+
+        def push(count):
+            arriving = owned.at[pl.ds(first, count)]
+
+            def send(k, _):
+                slot, target = route(k)
+                remote(nest.at[slot, pl.ds(0, count)], arriving, go_send, go_sem.at[r // 4], (d, target)).start()
+                return 0
+
+            lax.fori_loop(1, PER, send, 0)
+
+            @pl.when(owner == family)
+            def _():
+                pltpu.make_async_copy(nest.at[r * PER + place, pl.ds(0, count)], arriving, go_sem.at[r // 4]).start()
+
+            @pl.when(owner != family)
+            def _():
+                send(0, 0)
+
+        by_width(push)
 
     def orthogonalize(r):
         j = r // 4
         query = (1 - ids_ref[r * PER + place] % 2).astype(jnp.float32)
         width = VALUE_SCALE + query * (QUERY_SCALE - VALUE_SCALE)
-        drain(owned.at[j], go_sem.at[j])
-        block = owned[j].astype(jnp.float32)
-        rows = block.reshape(Q_IN, KV_OUT).astype(jnp.bfloat16)
+        base = j * 2 * X * Z * ALL
+        drain(owned.at[pl.ds(base, ARRIVING)], go_sem.at[j])
+        tiles = owned[pl.ds(base, 2 * X * Z * ALL)].astype(jnp.float32).reshape(2 * X * Z, ALL, 8, 128)
+        half = lax.broadcasted_iota(jnp.int32, (2 * X * Z - FULL, 8, 128), 2) < 64
+        folded = tiles[FULL:, 3]
+        narrow = [
+            jnp.where(half, folded, 0.0),
+            jnp.where(half, pltpu.roll(folded, 64, 2), 0.0),
+            tiles[FULL:, 4],
+        ]
+        right = jnp.concatenate([tiles[:FULL, 3:], jnp.stack(narrow, axis=1)], axis=0)
+        parts = [tiles[:, :3].reshape(Q_IN, 128), right.reshape(Q_IN, 128)]
+        rows = jnp.concatenate(parts, axis=1).astype(jnp.bfloat16)
         gram0 = lax.dot_general(rows, rows, (((0,), (0,)), ((), ())), preferred_element_type=jnp.float32)
         factor = polar_factor(gram0) * (width * step_rate)
         high, low = split(factor)
         result = dot(rows, high) + dot(rows, low)
-        back[j] = result.reshape(2 * X * Z, ROWS, KV_OUT).astype(jnp.bfloat16)
+        left = result[:, :128].reshape(2 * X * Z, 3, 8, 128)
+        right = result[:, 128:].reshape(2 * X * Z, 3, 8, 128)
+        narrow = right[FULL:]
+        folded = jnp.where(half, narrow[:, 0], pltpu.roll(narrow[:, 1], 64, 2))
+        packed = jnp.stack([folded, narrow[:, 2], narrow[:, 2]], axis=1)
+        tiles = jnp.concatenate([left, jnp.concatenate([right[:FULL], packed], axis=0)], axis=1)
+        back[pl.ds(base, 2 * X * Z * ALL)] = tiles.reshape(2 * X * Z * ALL, 8, 128).astype(jnp.bfloat16)
 
     def give(j, first, last):
         slot = (4 * j + family) * PER + place
 
         def send(k, _):
             target = 2 * X * ((z + k % Z) % Z) + (inner + k // Z) % (2 * X)
-            remote(back.at[j, target], update.at[slot], back_send, back_sem, (d, target)).start()
+
+            def push(count):
+                remote(
+                    back.at[pl.ds((j * 2 * X * Z + target) * ALL, count)], returned.at[slot, pl.ds(0, count)],
+                    back_send, back_sem.at[4 * j + family], (d, target),
+                ).start()
+
+            @pl.when(target < FULL)
+            def _():
+                push(ALL)
+
+            @pl.when(target >= FULL)
+            def _():
+                push(FEW)
+
             return 0
 
         lax.fori_loop(first, last, send, 0)
+
+    def keep(r):
+        def move(count):
+            pltpu.make_async_copy(
+                back.at[pl.ds(((r // 4) * 2 * X * Z + e) * ALL, count)],
+                returned.at[r * PER + place, pl.ds(0, count)],
+                back_sem.at[r],
+            ).start()
+
+        by_width(move)
+
+    def unpack(r):
+        drain_rows = pl.ds(r * PER, PER)
+
+        @pl.when(wide)
+        def _():
+            drain(returned.at[drain_rows], back_sem.at[r])
+
+            def one(i, _):
+                tiles = returned[r * PER + i].astype(jnp.float32)
+                update[r * PER + i] = jnp.concatenate(
+                    [tiles[:3].reshape(ROWS, 128), tiles[3:].reshape(ROWS, 128)], axis=1
+                ).astype(jnp.bfloat16)
+                return 0
+
+            lax.fori_loop(0, PER, one, 0, unroll=4)
+
+        @pl.when(jnp.logical_not(wide))
+        def _():
+            drain(returned.at[drain_rows, pl.ds(0, FEW)], back_sem.at[r])
+
+            def one(i, _):
+                tiles = returned[r * PER + i, pl.ds(0, FEW)].astype(jnp.float32)
+                first = jnp.where(lane < 64, tiles[3], 0.0)
+                second = jnp.where(lane < 64, pltpu.roll(tiles[3], 64, 1), 0.0)
+                right = jnp.concatenate([first, second, tiles[4]], axis=0)
+                update[r * PER + i] = jnp.concatenate(
+                    [tiles[:3].reshape(ROWS, 128), right], axis=1
+                ).astype(jnp.bfloat16)
+                return 0
+
+            lax.fori_loop(0, PER, one, 0, unroll=4)
 
     def given(t, start):
         paced = jnp.minimum(jnp.maximum(1 + (t - start + 1) * PACE, 1), 2 * X * Z)
@@ -230,14 +330,13 @@
         @pl.when(r % 4 == family)
         def _():
             orthogonalize(r)
-            pltpu.make_async_copy(back.at[r // 4, e], update.at[r * PER + place], back_sem).start()
+            keep(r)
 
         for j in range(2):
             start = LAG + 4 * j + family
             give(j, given(t - 1, start), given(t, start))
 
     relay(0)
-    relay(1)
     raw(0)
     load_logit.wait()
     for k in range(1, 2 * X):
@@ -248,6 +347,7 @@
     angle = jnp.full((1, KV_OUT), step_ref[0], jnp.int32).astype(jnp.float32) * (math.pi / plan_span)
     step_rate = 0.1 + 0.45 * (1.0 + jnp.cos(angle))
     combine(0)
+    relay(1)
     raw(1)
     relay(2)
     drain(peak_row, peak_sem.at[0])
@@ -257,9 +357,6 @@
     pltpu.make_async_copy(peak_a, peak_col.at[z], peak_sem.at[1]).start()
 
     for t in range(LAG):
-        combine(t + 1)
-        raw(t + 2)
-        relay(t + 3)
         home(t)
         if t == 0:
             drain(peak_col, peak_sem.at[1])
@@ -268,40 +365,51 @@
                 remote(peak_b, peak_dp.at[d], peak_send.at[2], peak_sem.at[2], (other, e)).start()
             pltpu.make_async_copy(peak_b, peak_dp.at[d], peak_sem.at[2]).start()
         go(t)
+        combine(t + 1)
+        raw(t + 2)
+        relay(t + 3)
 
     def step(t, _):
-        @pl.when(t + 1 < ROUNDS)
-        def _():
-            combine(t + 1)
-
-        @pl.when(t + 2 < ROUNDS)
-        def _():
-            raw(t + 2)
-
-        @pl.when(t + 3 < ROUNDS)
-        def _():
-            relay(t + 3)
-
         @pl.when(t < ROUNDS)
         def _():
             home(t)
             go(t)
 
+        @pl.when(t + 1 < ROUNDS)
+        def _():
+            combine(t + 1)
+
+        @pl.when(t + 2 < ROUNDS)
+        def _():
+            raw(t + 2)
+
+        @pl.when(t + 3 < ROUNDS)
+        def _():
+            relay(t + 3)
+
         finish(t)
         return 0
 
     lax.fori_loop(LAG, ROUNDS + LAG, step, 0)
 
+    def collect(r, _):
+        unpack(r)
+        return 0
+
+    lax.fori_loop(0, ROUNDS, collect, 0)
     drain(peak_dp, peak_sem.at[2])
     peaks_out[...] = jnp.max(peak_dp[...], axis=0)
     drain(peak_row.at[pl.ds(0, 2 * X - 1)], peak_send.at[0])
     drain(peak_col.at[pl.ds(0, Z - 1)], peak_send.at[1])
     drain(peak_dp.at[pl.ds(0, DP - 1)], peak_send.at[2])
     for sem in (relay_send, raw_send, sum_send):
-        drain(nest, sem)
-    drain(nest.at[pl.ds(0, SLOTS - 2)], go_send)
-    drain(nest.at[pl.ds(0, SLOTS - 2)], back_send)
-    drain(update, back_sem)
+        drain(held, sem)
+
+    def settle(count):
+        drain(nest.at[pl.ds(0, (SLOTS - 2) * count // ALL)], go_send)
+        drain(back.at[pl.ds(0, 2 * (ARRIVING - count))], back_send)
+
+    by_width(settle)
 
 
 def fused_step(ids, step, grads, momentum, logit):
@@ -310,7 +418,8 @@
     halves = pltpu.VMEM((ROUNDS, HALF) + slab, bf16)
     wholes = pltpu.VMEM((ROUNDS, 2, HALF) + slab, bf16)
     slots = pltpu.VMEM((SLOTS,) + slab, bf16)
-    pair = pltpu.VMEM((2, 2 * X * Z) + slab, bf16)
+    tiles = pltpu.VMEM((SLOTS, ALL, 8, 128), bf16)
+    flat = pltpu.VMEM((SLOTS * ALL, 8, 128), bf16)
     heads = logit.shape
     dma = pltpu.SemaphoreType.DMA
     vmem = pl.BlockSpec(memory_space=pltpu.VMEM)
@@ -327,13 +436,13 @@
         scratch_shapes=[
             pltpu.SMEM(ids.shape, jnp.int32),
             pltpu.VMEM(heads, jnp.float32),
-            wholes, halves, halves, slots, halves, halves, wholes, wholes, slots, pair, pair,
+            wholes, halves, halves, slots, halves, halves, wholes, wholes, tiles, flat, flat, tiles,
             pltpu.VMEM((2 * X,) + heads, jnp.float32),
             pltpu.VMEM((Z,) + heads, jnp.float32),
             pltpu.VMEM((DP,) + heads, jnp.float32),
             pltpu.VMEM(heads, jnp.float32),
             pltpu.VMEM(heads, jnp.float32),
-            dma((6,)), dma, dma((ROUNDS, 2)), dma, dma, dma((ROUNDS, 2)), dma, dma((2,)), dma, dma,
+            dma((6,)), dma, dma((ROUNDS, 2)), dma, dma, dma((ROUNDS, 2)), dma, dma((2,)), dma, dma((ROUNDS,)),
             dma((3,)), dma((3,)),
         ],
         compiler_params=pltpu.CompilerParams(

time: 105 us -> 101 us (0.962)
  Pallas kernels: 104 us -> 99.9 us
    pallas_call x1, Pallas kernels: 101 us -> 96.9 us  [fused_step(): pl.pallas_call(step_kernel, in_specs=[hbm, pl.BlockSpec(memory_space=pltp...]
where the time goes in v4:
time: 101 us
  Pallas kernels  99.9 us (99%)
  between operations  1.28 us (1%)
    pallas_call x1, Pallas kernels, fused_step(): pl.pallas_call(step_kernel, in_specs=[hbm, pl.BlockSpec(memory_space=pltp...  96.9 us
    pallas_call x1, Pallas kernels, write_out(): pl.pallas_call(tail_kernel, in_specs=[vmem, vmem, vmem, vmem], out_specs=...  2.99 us

profile of v4, /device:TPU:1, one launch (start us, length us, event | category | flops | bytes accessed | tf_op | source)
XLA Modules:
  0.0 101.2 jit_solution(2664164009942259948)
XLA Ops:
  1.3 96.9 %shard_map.76 = (bf16[128,24,256]{2,1,0:T(8,128)(2,1)S(1)}, bf16[128,24,256]{2,1,0:T(8,128)(2,1)S(1)}, f32[4,64]{1,0:T(4,128)S(1)}) custom-call(s32[128]{0:T(128)} %ids_hbm.1, s32[1]{0:T(128)S(6)} %copy.8.step_ref, bf16[4,8,2,8,24,256]{5,4,3,2,1,0:T(8,128)(2,1)} %bitcast.3, bf16[128,24,256]{2,1,0:T(8,128)(2,1)} %momentum.1, f32[4,64]{1,0:T(4,128)} %bitcast.4), custom_call_target="tpu_custom_call" | custom-call | tf_op jit(solution)/shard_map/pallas_call | solution.py:427
  98.2 3.0 %shard_map.77 = (bf16[128,24,256]{2,1,0:T(8,128)(2,1)}, bf16[128,24,256]{2,1,0:T(8,128)(2,1)}, f32[128,256]{1,0:T(8,128)}) custom-call(s32[1,128]{1,0:T(1,128)} %bitcast.5, f32[4,64]{1,0:T(4,128)S(1)} %get-tuple-element.6.peaks_ref, bf16[128,24,256]{2,1,0:T(8,128)(2,1)S(1)} %get-tuple-element.7.fresh, bf16[128,24,256]{2,1,0:T(8,128)(2,1)S(1)} %get-tuple-element.8.update), custom_call_target="tpu_custom_call" | custom-call | tf_op jit(solution)/shard_map/pallas_call | solution.py:481

commit v5 on v4

--- a/solution.py
+++ b/solution.py
@@ -79,8 +79,8 @@
 
 
 def step_kernel(
-    ids_hbm, step_ref, grads, momentum, logit_hbm, fresh, update, peaks_out,
-    ids_ref, logit,
+    ids_hbm, ids_row, step_ref, grads, momentum, logit_hbm, fresh, update, clip_ref,
+    ids_ref, ids_lane, logit,
     own, near_up, near_down, held, relay_up, relay_down, in_up, in_down, nest, owned, back, returned,
     peak_row, peak_col, peak_dp, peak_a, peak_b,
     load_sem, relay_send, relay_sem, raw_send, sum_send, in_sem, go_send, go_sem, back_send, back_sem,
@@ -90,7 +90,7 @@
     e = lax.axis_index("expert")
     z, x, core = e // (2 * X), (e // 2) % X, e % 2
     inner = e % (2 * X)
-    family = 2 * ((x + z) % 2) + core
+    family = (x + z) % 2 + 2 * core
     place = 2 * z + x // 2
     up, down, far = (d + 1) % DP, (d + 3) % DP, (d + 2) % DP
 
@@ -122,6 +122,7 @@
         pltpu.make_async_copy(grads.at[d], own, load_sem.at[2]),
         pltpu.make_async_copy(momentum, held, load_sem.at[3]),
         pltpu.make_async_copy(ids_hbm, ids_ref, load_sem.at[4]),
+        pltpu.make_async_copy(ids_row, ids_lane, load_sem.at[6]),
     ]
     load_logit = pltpu.make_async_copy(logit_hbm, logit, load_sem.at[5])
     load_logit.start()
@@ -195,14 +196,14 @@
 
             lax.fori_loop(0, HALF, one, 0, unroll=True)
 
-    def go(r):
+    def go(r, low, high):
         owner = r % 4
         first = (r // 4) * 2 * X * Z * ALL + e * ALL
 
         def route(k):
             to_z = (z + k % Z) % Z
             to_half = (x // 2 + k // Z) % 2
-            target = 2 * (X * to_z + 2 * to_half + (owner // 2 + to_z) % 2) + owner % 2
+            target = 2 * (X * to_z + 2 * to_half + (owner + to_z) % 2) + owner // 2
             return r * PER + 2 * to_z + to_half, target
 
         def push(count):
@@ -213,7 +214,9 @@
                 remote(nest.at[slot, pl.ds(0, count)], arriving, go_send, go_sem.at[r // 4], (d, target)).start()
                 return 0
 
-            lax.fori_loop(1, PER, send, 0)
+            lax.fori_loop(max(low, 1), high, send, 0)
+            if low > 0:
+                return
 
             @pl.when(owner == family)
             def _():
@@ -364,24 +367,32 @@
             for other in (up, down, far):
                 remote(peak_b, peak_dp.at[d], peak_send.at[2], peak_sem.at[2], (other, e)).start()
             pltpu.make_async_copy(peak_b, peak_dp.at[d], peak_sem.at[2]).start()
-        go(t)
         combine(t + 1)
+        go(t, 0, 8)
         raw(t + 2)
+        go(t, 8, PER)
         relay(t + 3)
 
     def step(t, _):
         @pl.when(t < ROUNDS)
         def _():
             home(t)
-            go(t)
 
         @pl.when(t + 1 < ROUNDS)
         def _():
             combine(t + 1)
 
+        @pl.when(t < ROUNDS)
+        def _():
+            go(t, 0, 8)
+
         @pl.when(t + 2 < ROUNDS)
         def _():
             raw(t + 2)
+
+        @pl.when(t < ROUNDS)
+        def _():
+            go(t, 8, PER)
 
         @pl.when(t + 3 < ROUNDS)
         def _():
@@ -391,14 +402,27 @@
         return 0
 
     lax.fori_loop(LAG, ROUNDS + LAG, step, 0)
+
+    drain(peak_dp, peak_sem.at[2])
+    eta = jnp.minimum(1.0, clip_tau / jnp.max(peak_dp[...], axis=0))
+    ids = jnp.transpose(jnp.broadcast_to(ids_lane[...], (SLOTS, SLOTS)))[:, 0:1]
+    kind = ids % 2
+    layer = ids // (2 * eta.shape[1])
+    head = (ids // 2) % eta.shape[1]
+    lanes = lax.broadcasted_iota(jnp.int32, (SLOTS, eta.shape[1]), 1)
+    picked = jnp.zeros((SLOTS, eta.shape[1]), jnp.float32)
+    for level in range(eta.shape[0]):
+        picked = jnp.where(layer == level, eta[level : level + 1, :], picked)
+    slot_eta = jnp.sum(jnp.where(lanes == head, picked, 0.0), axis=1, keepdims=True)
+    column = lax.broadcasted_iota(jnp.int32, (SLOTS, KV_OUT), 1)
+    rest = jnp.where(kind == 0, jnp.where(column < Q_OUT, slot_eta, 0.0), 1.0)
+    clip_ref[...] = jnp.where(column < NOPE_DIM, jnp.sqrt(slot_eta), rest)
 
     def collect(r, _):
         unpack(r)
         return 0
 
     lax.fori_loop(0, ROUNDS, collect, 0)
-    drain(peak_dp, peak_sem.at[2])
-    peaks_out[...] = jnp.max(peak_dp[...], axis=0)
     drain(peak_row.at[pl.ds(0, 2 * X - 1)], peak_send.at[0])
     drain(peak_col.at[pl.ds(0, Z - 1)], peak_send.at[1])
     drain(peak_dp.at[pl.ds(0, DP - 1)], peak_send.at[2])
@@ -412,7 +436,7 @@
     by_width(settle)
 
 
-def fused_step(ids, step, grads, momentum, logit):
+def fused_step(ids, ids_row, step, grads, momentum, logit):
     slab = (ROWS, KV_OUT)
     bf16 = jnp.bfloat16
     halves = pltpu.VMEM((ROUNDS, HALF) + slab, bf16)
@@ -426,15 +450,16 @@
     hbm = pl.BlockSpec(memory_space=pltpu.HBM)
     return pl.pallas_call(
         step_kernel,
-        in_specs=[hbm, pl.BlockSpec(memory_space=pltpu.SMEM), hbm, hbm, hbm],
+        in_specs=[hbm, hbm, pl.BlockSpec(memory_space=pltpu.SMEM), hbm, hbm, hbm],
         out_specs=[vmem, vmem, vmem],
         out_shape=[
             pltpu.VMEM((SLOTS,) + slab, bf16),
             pltpu.VMEM((SLOTS,) + slab, bf16),
-            pltpu.VMEM(heads, jnp.float32),
+            pltpu.VMEM((SLOTS, KV_OUT), jnp.float32),
         ],
         scratch_shapes=[
             pltpu.SMEM(ids.shape, jnp.int32),
+            pltpu.VMEM(ids_row.shape, jnp.int32),
             pltpu.VMEM(heads, jnp.float32),
             wholes, halves, halves, slots, halves, halves, wholes, wholes, tiles, flat, flat, tiles,
             pltpu.VMEM((2 * X,) + heads, jnp.float32),
@@ -442,63 +467,49 @@
             pltpu.VMEM((DP,) + heads, jnp.float32),
             pltpu.VMEM(heads, jnp.float32),
             pltpu.VMEM(heads, jnp.float32),
-            dma((6,)), dma, dma((ROUNDS, 2)), dma, dma, dma((ROUNDS, 2)), dma, dma((2,)), dma, dma((ROUNDS,)),
+            dma((7,)), dma, dma((ROUNDS, 2)), dma, dma, dma((ROUNDS, 2)), dma, dma((2,)), dma, dma((ROUNDS,)),
             dma((3,)), dma((3,)),
         ],
         compiler_params=pltpu.CompilerParams(
             collective_id=0, has_side_effects=True, vmem_limit_bytes=40 * 2**20
         ),
-    )(ids, step, grads, momentum, logit)
-
-
-def tail_kernel(ids_ref, peaks_ref, fresh, update, fresh_out, update_out, clip_ref, sems):
+    )(ids, ids_row, step, grads, momentum, logit)
+
+
+def tail_kernel(fresh, update, clip, fresh_out, update_out, clip_out, sems):
     copies = [
         pltpu.make_async_copy(fresh, fresh_out, sems.at[0]),
         pltpu.make_async_copy(update, update_out, sems.at[1]),
+        pltpu.make_async_copy(clip, clip_out, sems.at[2]),
     ]
     for copy in copies:
         copy.start()
-    eta = jnp.minimum(1.0, clip_tau / peaks_ref[...])
-    ids = jnp.transpose(jnp.broadcast_to(ids_ref[...], (SLOTS, SLOTS)))[:, 0:1]
-    kind = ids % 2
-    layer = ids // (2 * eta.shape[1])
-    head = (ids // 2) % eta.shape[1]
-    lanes = lax.broadcasted_iota(jnp.int32, (SLOTS, eta.shape[1]), 1)
-    picked = jnp.zeros((SLOTS, eta.shape[1]), jnp.float32)
-    for level in range(eta.shape[0]):
-        picked = jnp.where(layer == level, eta[level : level + 1, :], picked)
-    slot_eta = jnp.sum(jnp.where(lanes == head, picked, 0.0), axis=1, keepdims=True)
-    column = lax.broadcasted_iota(jnp.int32, (SLOTS, KV_OUT), 1)
-    rest = jnp.where(kind == 0, jnp.where(column < Q_OUT, slot_eta, 0.0), 1.0)
-    clip_ref[...] = jnp.where(column < NOPE_DIM, jnp.sqrt(slot_eta), rest)
     for copy in copies:
         copy.wait()
 
 
-def write_out(ids, peaks, fresh, update):
+def write_out(fresh, update, clip):
     vmem = pl.BlockSpec(memory_space=pltpu.VMEM)
     anywhere = pl.BlockSpec(memory_space=pl.ANY)
     return pl.pallas_call(
         tail_kernel,
-        in_specs=[vmem, vmem, vmem, vmem],
-        out_specs=[anywhere, anywhere, vmem],
+        in_specs=[vmem] * 3,
+        out_specs=[anywhere] * 3,
         out_shape=[
             jax.ShapeDtypeStruct(fresh.shape, fresh.dtype),
             jax.ShapeDtypeStruct(update.shape, update.dtype),
             jax.ShapeDtypeStruct((SLOTS, KV_OUT), jnp.float32),
         ],
-        scratch_shapes=[pltpu.SemaphoreType.DMA((2,))],
-    )(ids, peaks, fresh, update)
+        scratch_shapes=[pltpu.SemaphoreType.DMA((3,))],
+    )(fresh, update, clip)
 
 
 def body(grad_parts, momentum, block_ids, step, logit_max):
     grads = grad_parts.reshape(DP, ROUNDS, 2, HALF, ROWS, KV_OUT)
-    ids, grads, momentum, logit = (
-        pltpu.with_memory_space_constraint(a, pltpu.HBM) for a in (block_ids, grads, momentum, logit_max[0, 0])
-    )
-    results = fused_step(ids, step, grads, momentum, logit)
-    fresh, update, peaks = (pltpu.with_memory_space_constraint(a, pltpu.VMEM) for a in results)
-    return tuple(write_out(block_ids.reshape(1, SLOTS), peaks, fresh, update))
+    operands = (block_ids, block_ids.reshape(1, SLOTS), grads, momentum, logit_max[0, 0])
+    ids, ids_row, grads, momentum, logit = (pltpu.with_memory_space_constraint(a, pltpu.HBM) for a in operands)
+    results = fused_step(ids, ids_row, step, grads, momentum, logit)
+    return tuple(write_out(*(pltpu.with_memory_space_constraint(a, pltpu.VMEM) for a in results)))
 
 
 def solution(mesh):

time: 101 us -> 99.1 us (0.981)
  Pallas kernels: 99.9 us -> 97.8 us
    pallas_call x2, Pallas kernels: 99.9 us -> 97.8 us  [the longest x1 96 us: fused_step(): pl.pallas_call(step_kernel, in_specs=[hbm, hbm, pl.BlockSpec(memory_space...]
where the time goes in v5:
time: 99.1 us
  Pallas kernels  97.8 us (99%)
  between operations  1.29 us (1%)
    pallas_call x1, Pallas kernels, fused_step(): pl.pallas_call(step_kernel, in_specs=[hbm, hbm, pl.BlockSpec(memory_space...  96 us

profile of v5, /device:TPU:1, one launch (start us, length us, event | category | flops | bytes accessed | tf_op | source)
XLA Modules:
  0.0 99.1 jit_solution(4113295144224709349)
XLA Ops:
  1.3 96.0 %shard_map.76 = (bf16[128,24,256]{2,1,0:T(8,128)(2,1)S(1)}, bf16[128,24,256]{2,1,0:T(8,128)(2,1)S(1)}, f32[128,256]{1,0:T(8,128)S(1)}) custom-call(s32[128]{0:T(128)} %ids_hbm.1, s32[1,128]{1,0:T(1,128)} %bitcast.5, s32[1]{0:T(128)S(6)} %copy.8.step_ref, bf16[4,8,2,8,24,256]{5,4,3,2,1,0:T(8,128)(2,1)} %bitcast.3, bf16[128,24,256]{2,1,0:T(8,128)(2,1)} %momentum.1, ...), custom_call_target="tpu_custom_call" | custom-call | tf_op jit(solution)/shard_map/pallas_call | solution.py:451
  97.3 1.7 %shard_map.77 = (bf16[128,24,256]{2,1,0:T(8,128)(2,1)}, bf16[128,24,256]{2,1,0:T(8,128)(2,1)}, f32[128,256]{1,0:T(8,128)}) custom-call(bf16[128,24,256]{2,1,0:T(8,128)(2,1)S(1)} %get-tuple-element.6.fresh, bf16[128,24,256]{2,1,0:T(8,128)(2,1)S(1)} %get-tuple-element.7.update, f32[128,256]{1,0:T(8,128)S(1)} %get-tuple-element.8.clip), custom_call_target="tpu_custom_call" | custom-call | tf_op jit(solution)/shard_map/pallas_call | solution.py:494

commit v6 on v5

--- a/solution.py
+++ b/solution.py
@@ -327,16 +327,17 @@
         paced = jnp.minimum(jnp.maximum(1 + (t - start + 1) * PACE, 1), 2 * X * Z)
         return jnp.where(t < ROUNDS, paced, jnp.where(t < start, 1, 2 * X * Z))
 
+    starts = (LAG + family - jnp.where(family < 2, 1, 0), LAG + 5 + family)
+
     def finish(t):
-        r = t - LAG
-
-        @pl.when(r % 4 == family)
-        def _():
+        @pl.when((t == starts[0]) | (t == starts[1]))
+        def _():
+            r = 4 * jnp.where(t == starts[1], 1, 0) + family
             orthogonalize(r)
             keep(r)
 
         for j in range(2):
-            start = LAG + 4 * j + family
+            start = starts[j]
             give(j, given(t - 1, start), given(t, start))
 
     relay(0)
@@ -345,7 +346,7 @@
     for k in range(1, 2 * X):
         remote(logit, peak_row.at[inner], peak_send.at[0], peak_sem.at[0], (d, row_peer(k))).start()
     pltpu.make_async_copy(logit, peak_row.at[inner], peak_sem.at[0]).start()
-    for load in loads:
+    for load in loads[:2]:
         load.wait()
     angle = jnp.full((1, KV_OUT), step_ref[0], jnp.int32).astype(jnp.float32) * (math.pi / plan_span)
     step_rate = 0.1 + 0.45 * (1.0 + jnp.cos(angle))
@@ -359,7 +360,9 @@
         remote(peak_a, peak_col.at[z], peak_send.at[1], peak_sem.at[1], (d, column_peer(k))).start()
     pltpu.make_async_copy(peak_a, peak_col.at[z], peak_sem.at[1]).start()
 
-    for t in range(LAG):
+    for load in loads[2:]:
+        load.wait()
+    for t in range(1):
         home(t)
         if t == 0:
             drain(peak_col, peak_sem.at[1])
@@ -401,7 +404,7 @@
         finish(t)
         return 0
 
-    lax.fori_loop(LAG, ROUNDS + LAG, step, 0)
+    lax.fori_loop(1, ROUNDS + LAG + 1, step, 0)
 
     drain(peak_dp, peak_sem.at[2])
     eta = jnp.minimum(1.0, clip_tau / jnp.max(peak_dp[...], axis=0))

time: 99.1 us -> 96.2 us (0.971)
  Pallas kernels: 97.8 us -> 94.9 us
    pallas_call x1, Pallas kernels: 96 us -> 93.1 us  [fused_step(): pl.pallas_call(step_kernel, in_specs=[hbm, hbm, pl.BlockSpec(memory_space...]
where the time goes in v6:
time: 96.2 us; the launch traced here: 96.1 us
  Pallas kernels  94.9 us (99%)
  between operations  1.29 us (1%)
    pallas_call x1, Pallas kernels, fused_step(): pl.pallas_call(step_kernel, in_specs=[hbm, hbm, pl.BlockSpec(memory_space...  93.1 us

profile of v6, /device:TPU:1, one launch (start us, length us, event | category | flops | bytes accessed | tf_op | source)
XLA Modules:
  0.0 96.1 jit_solution(16075507990384348080)
XLA Ops:
  1.3 93.1 %shard_map.76 = (bf16[128,24,256]{2,1,0:T(8,128)(2,1)S(1)}, bf16[128,24,256]{2,1,0:T(8,128)(2,1)S(1)}, f32[128,256]{1,0:T(8,128)S(1)}) custom-call(s32[128]{0:T(128)} %ids_hbm.1, s32[1,128]{1,0:T(1,128)} %bitcast.5, s32[1]{0:T(128)S(6)} %copy.8.step_ref, bf16[4,8,2,8,24,256]{5,4,3,2,1,0:T(8,128)(2,1)} %bitcast.3, bf16[128,24,256]{2,1,0:T(8,128)(2,1)} %momentum.1, ...), custom_call_target="tpu_custom_call" | custom-call | tf_op jit(solution)/shard_map/pallas_call | solution.py:454
  94.4 1.7 %shard_map.77 = (bf16[128,24,256]{2,1,0:T(8,128)(2,1)}, bf16[128,24,256]{2,1,0:T(8,128)(2,1)}, f32[128,256]{1,0:T(8,128)}) custom-call(bf16[128,24,256]{2,1,0:T(8,128)(2,1)S(1)} %get-tuple-element.6.fresh, bf16[128,24,256]{2,1,0:T(8,128)(2,1)S(1)} %get-tuple-element.7.update, f32[128,256]{1,0:T(8,128)S(1)} %get-tuple-element.8.clip), custom_call_target="tpu_custom_call" | custom-call | tf_op jit(solution)/shard_map/pallas_call | solution.py:497

commit v7 on v6

--- a/solution.py
+++ b/solution.py
@@ -214,7 +214,7 @@
                 remote(nest.at[slot, pl.ds(0, count)], arriving, go_send, go_sem.at[r // 4], (d, target)).start()
                 return 0
 
-            lax.fori_loop(max(low, 1), high, send, 0)
+            lax.fori_loop(max(low, 1), high, send, 0, unroll=True)
             if low > 0:
                 return
 
@@ -370,8 +370,8 @@
             for other in (up, down, far):
                 remote(peak_b, peak_dp.at[d], peak_send.at[2], peak_sem.at[2], (other, e)).start()
             pltpu.make_async_copy(peak_b, peak_dp.at[d], peak_sem.at[2]).start()
+        go(t, 0, 8)
         combine(t + 1)
-        go(t, 0, 8)
         raw(t + 2)
         go(t, 8, PER)
         relay(t + 3)
@@ -381,13 +381,13 @@
         def _():
             home(t)
 
+        @pl.when(t < ROUNDS)
+        def _():
+            go(t, 0, 8)
+
         @pl.when(t + 1 < ROUNDS)
         def _():
             combine(t + 1)
-
-        @pl.when(t < ROUNDS)
-        def _():
-            go(t, 0, 8)
 
         @pl.when(t + 2 < ROUNDS)
         def _():

time: 96.2 us -> 96.1 us (level)
  no operation moved by 1% of the time
where the time goes in v7:
time: 96.1 us; the launch traced here: 96 us
  Pallas kernels  94.7 us (99%)
  between operations  1.29 us (1%)
    pallas_call x1, Pallas kernels, fused_step(): pl.pallas_call(step_kernel, in_specs=[hbm, hbm, pl.BlockSpec(memory_space...  93 us

profile of v7, /device:TPU:1, one launch (start us, length us, event | category | flops | bytes accessed | tf_op | source)
XLA Modules:
  0.0 96.0 jit_solution(976577295548274638)
XLA Ops:
  1.3 93.0 %shard_map.76 = (bf16[128,24,256]{2,1,0:T(8,128)(2,1)S(1)}, bf16[128,24,256]{2,1,0:T(8,128)(2,1)S(1)}, f32[128,256]{1,0:T(8,128)S(1)}) custom-call(s32[128]{0:T(128)} %ids_hbm.1, s32[1,128]{1,0:T(1,128)} %bitcast.5, s32[1]{0:T(128)S(6)} %copy.8.step_ref, bf16[4,8,2,8,24,256]{5,4,3,2,1,0:T(8,128)(2,1)} %bitcast.3, bf16[128,24,256]{2,1,0:T(8,128)(2,1)} %momentum.1, ...), custom_call_target="tpu_custom_call" | custom-call | tf_op jit(solution)/shard_map/pallas_call | solution.py:454
  94.3 1.7 %shard_map.77 = (bf16[128,24,256]{2,1,0:T(8,128)(2,1)}, bf16[128,24,256]{2,1,0:T(8,128)(2,1)}, f32[128,256]{1,0:T(8,128)}) custom-call(bf16[128,24,256]{2,1,0:T(8,128)(2,1)S(1)} %get-tuple-element.6.fresh, bf16[128,24,256]{2,1,0:T(8,128)(2,1)S(1)} %get-tuple-element.7.update, f32[128,256]{1,0:T(8,128)S(1)} %get-tuple-element.8.clip), custom_call_target="tpu_custom_call" | custom-call | tf_op jit(solution)/shard_map/pallas_call | solution.py:497
